TPU v7x, 32 devices: a whole 2x2x4 slice. The times are simulated.
32 devices in a mesh: ctx: 8 (over y, x, core), head: 4 (over z).
Axes of the slice: x: 2, y: 2, z: 4, core: 2. Of those that a mesh axis runs over, the one named last changes fastest.
Arguments:
- queries: bfloat16 [3072, 8192], P('ctx', 'head')
- query_scale: bfloat16 [3072, 64], P('ctx', 'head'), may hold values from 0.25 to 4
- keys: bfloat16 [3072, 1024], P('ctx', 'head')
- key_scale: bfloat16 [3072, 8], P('ctx', 'head'), may hold values from 0.4 to 2
- values: bfloat16 [3072, 1024], P('ctx', 'head'), may hold values from -6 to 6
- value_scale: bfloat16 [3072, 8], P('ctx', 'head'), may hold values from 0.5 to 2
- block_mask: int32 [24, 24], replicated, may hold values from 0 to 1, as said below
- out_weight: bfloat16 [8192, 8192], P('head'), may hold values from -0.5 to 0.5
- out_scale: float32 [8192], P('head'), may hold values from 0.5 to 2
Outputs:
- output: bfloat16 [3072, 8192], P('ctx', 'head')
Inputs may be any that keep to these rules, and one draw needn't show every extreme that they name: block_mask[i, j] is 0 for j > i and 1 for j = i.
All inputs are finite; a program needn't handle non-finite values.
Results may differ from a plain program's by a relative error of at most 0.02.
Values may be sent and summed in bfloat16 or wider, within the bound.
A program may use at most 128 MiB of HBM per device.

v0:
```python
import math

import jax
import jax.numpy as jnp
from jax import lax
from jax.sharding import PartitionSpec as P

HD = 128
GROUP = 8
BLK = 128


NEG_FILL = -1e30


def block_rows(positions, mask_table):
    count = mask_table.shape[0]
    table_hot = (positions[:, None] // BLK == jnp.arange(count, dtype=jnp.int32)[None, :]).astype(
        jnp.float32
    )
    return jnp.dot(table_hot, mask_table.astype(jnp.float32))


def make_set(q_rows, q_scales, positions, mask_table, limit):
    count = q_rows.shape[0]
    kv_local = q_rows.shape[1] // (GROUP * HD)
    shaped = q_rows.reshape(count, kv_local, GROUP, HD)
    factors = jnp.transpose(q_scales.astype(jnp.float32).reshape(count, kv_local, GROUP), (1, 2, 0))
    return (shaped, factors, positions, block_rows(positions, mask_table), limit)


def attend_block(state, query_set, key_rows, key_scales, value_rows, value_scales, first_key):
    q_rows, factors, positions, mask_rows, limit = query_set
    top, total, accum = state
    kv_local = q_rows.shape[1]
    width = key_rows.shape[0]
    keys3 = key_rows.reshape(width, kv_local, HD)
    vals3 = value_rows.reshape(width, kv_local, HD)
    key_pos = first_key + jnp.arange(width, dtype=jnp.int32)
    col_hot = (
        key_pos[:, None] // BLK == jnp.arange(mask_rows.shape[1], dtype=jnp.int32)[None, :]
    ).astype(jnp.float32)
    block_ok = jnp.dot(mask_rows, col_hot.T) > 0.5
    allowed = block_ok & (key_pos[None, :] <= positions[:, None])
    inv_root = 1.0 / jnp.sqrt(jnp.float32(HD))
    raw = jnp.einsum("rkgd,nkd->kgrn", q_rows, keys3, preferred_element_type=jnp.float32)
    scores = (
        raw * factors[..., None] * key_scales.astype(jnp.float32).T[:, None, None, :] * inv_root
    )
    scores = jnp.where(allowed[None, None], scores, NEG_FILL)
    new_top = jnp.maximum(top, jnp.max(scores, axis=3))
    expo = jnp.where(allowed[None, None], jnp.exp(scores - new_top[..., None]), 0.0)
    decay = jnp.exp(top - new_top)
    weights = (expo * value_scales.astype(jnp.float32).T[:, None, None, :]).astype(jnp.bfloat16)
    total = total * decay + jnp.sum(expo, axis=3)
    accum = accum * decay[..., None] + jnp.einsum(
        "kgrn,nkd->kgrd", weights, vals3, preferred_element_type=jnp.float32
    )
    return (new_top, total, accum)


def empty_state(query_set):
    q_rows = query_set[0]
    count, kv_local = (q_rows.shape[0], q_rows.shape[1])
    top = jnp.full((kv_local, GROUP, count), NEG_FILL, jnp.float32)
    total = jnp.zeros((kv_local, GROUP, count), jnp.float32)
    accum = jnp.zeros((kv_local, GROUP, count, HD), jnp.float32)
    return (top, total, accum)


def finish_state(state):
    top, total, accum = state
    kv_local, count = (accum.shape[0], accum.shape[2])
    safe_total = jnp.where(total > 0.0, total, 1.0)
    attended = accum / safe_total[..., None]
    return (
        jnp.transpose(attended, (2, 0, 1, 3))
        .reshape(count, kv_local * GROUP * HD)
        .astype(jnp.bfloat16)
    )


def run_attention(query_sets, keys, key_scale, values, value_scale):

    def fold_piece(states, key_piece, first_key):
        key_rows, key_sc, value_rows, value_sc = key_piece
        width = key_rows.shape[0]
        span = math.gcd(width, 512)

        def one_set(state, query_set):

            def compute(st_begin):

                def inner(i, st_now):
                    offset = i * span
                    return attend_block(
                        st_now,
                        query_set,
                        lax.dynamic_slice_in_dim(key_rows, offset, span, 0),
                        lax.dynamic_slice_in_dim(key_sc, offset, span, 0),
                        lax.dynamic_slice_in_dim(value_rows, offset, span, 0),
                        lax.dynamic_slice_in_dim(value_sc, offset, span, 0),
                        offset,
                    )

                return lax.fori_loop(0, width // span, inner, st_begin)

            def unchanged(st_begin):
                return st_begin

            return lax.cond(first_key <= query_set[4], compute, unchanged, state)

        return tuple((one_set(state, query_set) for state, query_set in zip(states, query_sets)))

    starting = tuple((empty_state(query_set) for query_set in query_sets))
    states = fold_piece(
        starting,
        (
            lax.all_gather(keys, "ctx", axis=0, tiled=True),
            lax.all_gather(key_scale, "ctx", axis=0, tiled=True),
            lax.all_gather(values, "ctx", axis=0, tiled=True),
            lax.all_gather(value_scale, "ctx", axis=0, tiled=True),
        ),
        jnp.int32(0),
    )
    return tuple((finish_state(state) for state in states))


def local(
    queries, query_scale, keys, key_scale, values, value_scale, block_mask, out_weight, out_scale
):
    tok_rows = queries.shape[0]
    ctx_rank = lax.axis_index("ctx")
    first_own = ctx_rank * tok_rows
    own_pos = first_own + jnp.arange(tok_rows, dtype=jnp.int32)
    whole_set = make_set(queries, query_scale, own_pos, block_mask, first_own + tok_rows - 1)
    (attended,) = run_attention((whole_set,), keys, key_scale, values, value_scale)
    projected = jnp.dot(attended, out_weight, preferred_element_type=jnp.float32)
    summed = lax.psum_scatter(
        projected.astype(jnp.bfloat16), "head", scatter_dimension=1, tiled=True
    ).astype(jnp.float32)
    return (summed * out_scale[None, :]).astype(jnp.bfloat16)


def solution(mesh):
    return jax.shard_map(
        local,
        mesh=mesh,
        in_specs=(
            P("ctx", "head"),
            P("ctx", "head"),
            P("ctx", "head"),
            P("ctx", "head"),
            P("ctx", "head"),
            P("ctx", "head"),
            P(),
            P("head", None),
            P("head"),
        ),
        out_specs=P("ctx", "head"),
        check_vma=False,
    )
```

profile of v0, /device:TPU:6, one launch (start us, length us, event | category | flops | bytes accessed | tf_op | source)
XLA Modules:
  0.0 334.2 jit_solution(4861609946343318254)
XLA Ops:
  6.5 1.7 copy.16
  8.3 0.0 all-gather.3.cloned.1.call-update
  8.3 0.0 all-gather.5.cloned.1.call-start
  8.4 1.7 copy.17
  10.1 0.0 all-gather.5.cloned.1.call-update
  10.1 0.0 reduce-scatter.2.cloned.1.call-start
  10.2 8.0 %all_gather.13 = bf16[3072,2]{0,1:T(2,128)(2,1)S(1)} all-gather(bf16[384,2]{0,1:T(2,128)(2,1)} %param.16), channel_id=1, replica_groups=mesh['ctx'=8,'head'=4] {'ctx'}, dimensions={0}, use_global_device_ids=true | all-gather | bytes 13824 | tf_op jit(solution)/shard_map/all_gather | solution.py:120
  18.2 8.8 %all_gather.14 = bf16[3072,2]{0,1:T(2,128)(2,1)S(1)} all-gather(bf16[384,2]{0,1:T(2,128)(2,1)} %param.18), channel_id=1, replica_groups=mesh['ctx'=8,'head'=4] {'ctx'}, dimensions={0}, use_global_device_ids=true | all-gather | bytes 13824 | tf_op jit(solution)/shard_map/all_gather | solution.py:122
  27.0 1.0 fusion.18
  27.9 0.7 convert_bitcast_fusion.2
  28.6 6.8 %all-gather.3.cloned.1.call-done = bf16[3072,256]{0,1:T(8,128)(2,1)} async-done(((bf16[384,256]{0,1:T(8,128)(2,1)}), bf16[3072,256]{0,1:T(8,128)(2,1)}) %all-gather.3.cloned.1.call-update) | async-done | bytes 1572880 | tf_op jit(solution)/shard_map/all_gather | solution.py:119
  35.4 27.8 %all-gather.5.cloned.1.call-done = bf16[3072,256]{0,1:T(8,128)(2,1)} async-done(((bf16[384,256]{0,1:T(8,128)(2,1)}), bf16[3072,256]{0,1:T(8,128)(2,1)}) %all-gather.5.cloned.1.call-update) | async-done | bytes 1572880 | tf_op jit(solution)/shard_map/all_gather | solution.py:121
  63.2 127.2 %conditional.1 = (f32[2,8,384]{2,1,0:T(8,128)}, f32[2,8,384,128]{2,3,1,0:T(8,128)S(1)}) conditional(s32[]{:T(128)} %convert_element_type.55, () %tuple.35, (s32[]{:T(128)}, s32[384]{0:T(512)S(1)}, bf16[384,2048]{1,0:T(8,128)(2,1)}, bf16[384,24]{0,1:T(8,128)(2,1)S(1)}, bf16[3072,256]{0,1:T(8,128)(2,1)}, /*index=5*/f32[2,8,384]{2,1,0:T(8,128)S(1)}, ...), branch_computations={%region_0.1_spmd, %region_1.6_spmd} | conditional | flops 1685967232 | bytes 86248368 | solution.py:111
  63.2 1.9 copy.18
  65.1 1.6 copy.15
  66.7 121.3 %while.19 = (s32[]{:T(128)}, f32[2,8,384]{2,1,0:T(8,128)S(1)}, f32[2,8,384]{2,1,0:T(8,128)}, f32[2,8,384,128]{3,2,1,0:T(8,128)}, bf16[384,24]{0,1:T(8,128)(2,1)S...) while((s32[]{:T(128)}, f32[2,8,384]{2,1,0:T(8,128)S(1)}, ...), condition=%wide.region_5.5_spmd.clone, body=%wide.region_2.4_spmd.clone.sunk | while | flops 1685966848 | bytes 73662232 | solution.py:106
  66.7 0.3 fusion.43
  67.1 1.1 constant_dynamic-slice_fusion.3
  68.2 5.0 %fusion.44 = (f32[2,8,384]{2,1,0:T(8,128)S(1)}, f32[2,512,384,8]{2,1,3,0:T(8,128)S(1)}) fusion(f32[2,512]{1,0:T(2,128)S(1)} %get-tuple-element.507, f32[2,8,384]{2,1,0:T(8,128)S(1)} %get-tuple-element.557, pred[384,512]{0,1:T(8,128)(4,1)S(1)} %fusion.43, bf16[512,2,128,1]{0,2,3,1:T(8,128)(2,1)S(1)} %bitcast.73, ...), kind=kOutput, calls=%fused_computation.7.clone.1 | convolution fusion | flops 821028864 | bytes 14667776 | tf_op jit(solution)/shard_map/cond/branch_1_fun/while/body/eval_jaxpr/rkgd,nkd->kgrn/dot_general | solution.py:46
  73.2 4.1 %fusion.45 = f32[2,8,384]{2,1,0:T(8,128)S(1)} fusion(f32[2,512,384,8]{2,1,3,0:T(8,128)S(1)} %get-tuple-element.512, f32[2,8,384]{2,1,0:T(8,128)S(1)} %select_maximum_fusion.2, f32[2,512]{1,0:T(2,128)S(1)} %get-tuple-element.507, f32[2,8,384]{2,1,0:T(8,128)S(1)} %get-tuple-element.557, pred[384,512]{0,1:T(8,128)(4,1)S(1)} %fusion.43), kind=kLoop, calls=%fused_computation.6.clone.1 | loop fusion | flops 22013952 | bytes 12857344 | tf_op jit(solution)/shard_map/cond/branch_1_fun/while/body/eval_jaxpr/reduce_sum | solution.py:55
  77.3 0.6 fusion.46
  77.9 6.7 %fusion.47 = f32[2,8,384,128]{3,2,1,0:T(8,128)S(1)} fusion(f32[2,8,384,128]{3,2,1,0:T(8,128)S(1)} %copy-done, bf16[512,2,128,1]{0,2,3,1:T(8,128)(2,1)S(1)} %bitcast.72, f32[2,512,384,8]{2,1,3,0:T(8,128)S(1)} %get-tuple-element.512, f32[2,512]{1,0:T(2,128)S(1)} %get-tuple-element.515, f32[2,8,384]{2,1,0:T(8,128)S(1)} %select_maximum_fusion.2, ...), kind=kOutput, calls=%fused_computation.11.clone.1 | convolution fusion | flops 832831488 | bytes 19415040 | tf_op jit(solution)/shard_map/cond/branch_1_fun/while/body/eval_jaxpr/kgrn,nkd->kgrd/dot_general | solution.py:56
  84.7 1.6 copy-done.1
  86.3 0.4 fusion.43
  86.7 1.1 constant_dynamic-slice_fusion.3
  87.8 5.0 %fusion.44 = (f32[2,8,384]{2,1,0:T(8,128)S(1)}, f32[2,512,384,8]{2,1,3,0:T(8,128)S(1)}) fusion(f32[2,512]{1,0:T(2,128)S(1)} %get-tuple-element.507, f32[2,8,384]{2,1,0:T(8,128)S(1)} %get-tuple-element.557, pred[384,512]{0,1:T(8,128)(4,1)S(1)} %fusion.43, bf16[512,2,128,1]{0,2,3,1:T(8,128)(2,1)S(1)} %bitcast.73, ...), kind=kOutput, calls=%fused_computation.7.clone.1 | convolution fusion | flops 821028864 | bytes 14667776 | tf_op jit(solution)/shard_map/cond/branch_1_fun/while/body/eval_jaxpr/rkgd,nkd->kgrn/dot_general | solution.py:46
  92.8 4.1 %fusion.45 = f32[2,8,384]{2,1,0:T(8,128)S(1)} fusion(f32[2,512,384,8]{2,1,3,0:T(8,128)S(1)} %get-tuple-element.512, f32[2,8,384]{2,1,0:T(8,128)S(1)} %select_maximum_fusion.2, f32[2,512]{1,0:T(2,128)S(1)} %get-tuple-element.507, f32[2,8,384]{2,1,0:T(8,128)S(1)} %get-tuple-element.557, pred[384,512]{0,1:T(8,128)(4,1)S(1)} %fusion.43), kind=kLoop, calls=%fused_computation.6.clone.1 | loop fusion | flops 22013952 | bytes 12857344 | tf_op jit(solution)/shard_map/cond/branch_1_fun/while/body/eval_jaxpr/reduce_sum | solution.py:55
  96.9 1.4 fusion.46
  98.3 6.7 %fusion.47 = f32[2,8,384,128]{3,2,1,0:T(8,128)S(1)} fusion(f32[2,8,384,128]{3,2,1,0:T(8,128)S(1)} %copy-done, bf16[512,2,128,1]{0,2,3,1:T(8,128)(2,1)S(1)} %bitcast.72, f32[2,512,384,8]{2,1,3,0:T(8,128)S(1)} %get-tuple-element.512, f32[2,512]{1,0:T(2,128)S(1)} %get-tuple-element.515, f32[2,8,384]{2,1,0:T(8,128)S(1)} %select_maximum_fusion.2, ...), kind=kOutput, calls=%fused_computation.11.clone.1 | convolution fusion | flops 832831488 | bytes 19415040 | tf_op jit(solution)/shard_map/cond/branch_1_fun/while/body/eval_jaxpr/kgrn,nkd->kgrd/dot_general | solution.py:56
  105.0 1.6 copy-done.1
  106.7 0.4 fusion.43
  107.0 1.1 constant_dynamic-slice_fusion.3
  108.1 5.0 %fusion.44 = (f32[2,8,384]{2,1,0:T(8,128)S(1)}, f32[2,512,384,8]{2,1,3,0:T(8,128)S(1)}) fusion(f32[2,512]{1,0:T(2,128)S(1)} %get-tuple-element.507, f32[2,8,384]{2,1,0:T(8,128)S(1)} %get-tuple-element.557, pred[384,512]{0,1:T(8,128)(4,1)S(1)} %fusion.43, bf16[512,2,128,1]{0,2,3,1:T(8,128)(2,1)S(1)} %bitcast.73, ...), kind=kOutput, calls=%fused_computation.7.clone.1 | convolution fusion | flops 821028864 | bytes 14667776 | tf_op jit(solution)/shard_map/cond/branch_1_fun/while/body/eval_jaxpr/rkgd,nkd->kgrn/dot_general | solution.py:46
  113.1 4.1 %fusion.45 = f32[2,8,384]{2,1,0:T(8,128)S(1)} fusion(f32[2,512,384,8]{2,1,3,0:T(8,128)S(1)} %get-tuple-element.512, f32[2,8,384]{2,1,0:T(8,128)S(1)} %select_maximum_fusion.2, f32[2,512]{1,0:T(2,128)S(1)} %get-tuple-element.507, f32[2,8,384]{2,1,0:T(8,128)S(1)} %get-tuple-element.557, pred[384,512]{0,1:T(8,128)(4,1)S(1)} %fusion.43), kind=kLoop, calls=%fused_computation.6.clone.1 | loop fusion | flops 22013952 | bytes 12857344 | tf_op jit(solution)/shard_map/cond/branch_1_fun/while/body/eval_jaxpr/reduce_sum | solution.py:55
  117.2 1.4 fusion.46
  118.6 6.7 %fusion.47 = f32[2,8,384,128]{3,2,1,0:T(8,128)S(1)} fusion(f32[2,8,384,128]{3,2,1,0:T(8,128)S(1)} %copy-done, bf16[512,2,128,1]{0,2,3,1:T(8,128)(2,1)S(1)} %bitcast.72, f32[2,512,384,8]{2,1,3,0:T(8,128)S(1)} %get-tuple-element.512, f32[2,512]{1,0:T(2,128)S(1)} %get-tuple-element.515, f32[2,8,384]{2,1,0:T(8,128)S(1)} %select_maximum_fusion.2, ...), kind=kOutput, calls=%fused_computation.11.clone.1 | convolution fusion | flops 832831488 | bytes 19415040 | tf_op jit(solution)/shard_map/cond/branch_1_fun/while/body/eval_jaxpr/kgrn,nkd->kgrd/dot_general | solution.py:56
  125.4 1.6 copy-done.1
  127.0 0.4 fusion.43
  127.4 1.1 constant_dynamic-slice_fusion.3
  128.4 5.0 %fusion.44 = (f32[2,8,384]{2,1,0:T(8,128)S(1)}, f32[2,512,384,8]{2,1,3,0:T(8,128)S(1)}) fusion(f32[2,512]{1,0:T(2,128)S(1)} %get-tuple-element.507, f32[2,8,384]{2,1,0:T(8,128)S(1)} %get-tuple-element.557, pred[384,512]{0,1:T(8,128)(4,1)S(1)} %fusion.43, bf16[512,2,128,1]{0,2,3,1:T(8,128)(2,1)S(1)} %bitcast.73, ...), kind=kOutput, calls=%fused_computation.7.clone.1 | convolution fusion | flops 821028864 | bytes 14667776 | tf_op jit(solution)/shard_map/cond/branch_1_fun/while/body/eval_jaxpr/rkgd,nkd->kgrn/dot_general | solution.py:46
  133.5 4.1 %fusion.45 = f32[2,8,384]{2,1,0:T(8,128)S(1)} fusion(f32[2,512,384,8]{2,1,3,0:T(8,128)S(1)} %get-tuple-element.512, f32[2,8,384]{2,1,0:T(8,128)S(1)} %select_maximum_fusion.2, f32[2,512]{1,0:T(2,128)S(1)} %get-tuple-element.507, f32[2,8,384]{2,1,0:T(8,128)S(1)} %get-tuple-element.557, pred[384,512]{0,1:T(8,128)(4,1)S(1)} %fusion.43), kind=kLoop, calls=%fused_computation.6.clone.1 | loop fusion | flops 22013952 | bytes 12857344 | tf_op jit(solution)/shard_map/cond/branch_1_fun/while/body/eval_jaxpr/reduce_sum | solution.py:55
  137.6 1.4 fusion.46
  138.9 6.7 %fusion.47 = f32[2,8,384,128]{3,2,1,0:T(8,128)S(1)} fusion(f32[2,8,384,128]{3,2,1,0:T(8,128)S(1)} %copy-done, bf16[512,2,128,1]{0,2,3,1:T(8,128)(2,1)S(1)} %bitcast.72, f32[2,512,384,8]{2,1,3,0:T(8,128)S(1)} %get-tuple-element.512, f32[2,512]{1,0:T(2,128)S(1)} %get-tuple-element.515, f32[2,8,384]{2,1,0:T(8,128)S(1)} %select_maximum_fusion.2, ...), kind=kOutput, calls=%fused_computation.11.clone.1 | convolution fusion | flops 832831488 | bytes 19415040 | tf_op jit(solution)/shard_map/cond/branch_1_fun/while/body/eval_jaxpr/kgrn,nkd->kgrd/dot_general | solution.py:56
  145.7 1.6 copy-done.1
  147.3 0.4 fusion.43
  147.7 1.1 constant_dynamic-slice_fusion.3
  148.8 5.0 %fusion.44 = (f32[2,8,384]{2,1,0:T(8,128)S(1)}, f32[2,512,384,8]{2,1,3,0:T(8,128)S(1)}) fusion(f32[2,512]{1,0:T(2,128)S(1)} %get-tuple-element.507, f32[2,8,384]{2,1,0:T(8,128)S(1)} %get-tuple-element.557, pred[384,512]{0,1:T(8,128)(4,1)S(1)} %fusion.43, bf16[512,2,128,1]{0,2,3,1:T(8,128)(2,1)S(1)} %bitcast.73, ...), kind=kOutput, calls=%fused_computation.7.clone.1 | convolution fusion | flops 821028864 | bytes 14667776 | tf_op jit(solution)/shard_map/cond/branch_1_fun/while/body/eval_jaxpr/rkgd,nkd->kgrn/dot_general | solution.py:46
  153.8 4.1 %fusion.45 = f32[2,8,384]{2,1,0:T(8,128)S(1)} fusion(f32[2,512,384,8]{2,1,3,0:T(8,128)S(1)} %get-tuple-element.512, f32[2,8,384]{2,1,0:T(8,128)S(1)} %select_maximum_fusion.2, f32[2,512]{1,0:T(2,128)S(1)} %get-tuple-element.507, f32[2,8,384]{2,1,0:T(8,128)S(1)} %get-tuple-element.557, pred[384,512]{0,1:T(8,128)(4,1)S(1)} %fusion.43), kind=kLoop, calls=%fused_computation.6.clone.1 | loop fusion | flops 22013952 | bytes 12857344 | tf_op jit(solution)/shard_map/cond/branch_1_fun/while/body/eval_jaxpr/reduce_sum | solution.py:55
  157.9 1.4 fusion.46
  159.3 6.7 %fusion.47 = f32[2,8,384,128]{3,2,1,0:T(8,128)S(1)} fusion(f32[2,8,384,128]{3,2,1,0:T(8,128)S(1)} %copy-done, bf16[512,2,128,1]{0,2,3,1:T(8,128)(2,1)S(1)} %bitcast.72, f32[2,512,384,8]{2,1,3,0:T(8,128)S(1)} %get-tuple-element.512, f32[2,512]{1,0:T(2,128)S(1)} %get-tuple-element.515, f32[2,8,384]{2,1,0:T(8,128)S(1)} %select_maximum_fusion.2, ...), kind=kOutput, calls=%fused_computation.11.clone.1 | convolution fusion | flops 832831488 | bytes 19415040 | tf_op jit(solution)/shard_map/cond/branch_1_fun/while/body/eval_jaxpr/kgrn,nkd->kgrd/dot_general | solution.py:56
  166.0 1.6 copy-done.1
  167.7 0.4 fusion.43
  168.0 1.1 constant_dynamic-slice_fusion.3
  169.1 5.0 %fusion.44 = (f32[2,8,384]{2,1,0:T(8,128)S(1)}, f32[2,512,384,8]{2,1,3,0:T(8,128)S(1)}) fusion(f32[2,512]{1,0:T(2,128)S(1)} %get-tuple-element.507, f32[2,8,384]{2,1,0:T(8,128)S(1)} %get-tuple-element.557, pred[384,512]{0,1:T(8,128)(4,1)S(1)} %fusion.43, bf16[512,2,128,1]{0,2,3,1:T(8,128)(2,1)S(1)} %bitcast.73, ...), kind=kOutput, calls=%fused_computation.7.clone.1 | convolution fusion | flops 821028864 | bytes 14667776 | tf_op jit(solution)/shard_map/cond/branch_1_fun/while/body/eval_jaxpr/rkgd,nkd->kgrn/dot_general | solution.py:46
  174.1 4.1 %fusion.45 = f32[2,8,384]{2,1,0:T(8,128)S(1)} fusion(f32[2,512,384,8]{2,1,3,0:T(8,128)S(1)} %get-tuple-element.512, f32[2,8,384]{2,1,0:T(8,128)S(1)} %select_maximum_fusion.2, f32[2,512]{1,0:T(2,128)S(1)} %get-tuple-element.507, f32[2,8,384]{2,1,0:T(8,128)S(1)} %get-tuple-element.557, pred[384,512]{0,1:T(8,128)(4,1)S(1)} %fusion.43), kind=kLoop, calls=%fused_computation.6.clone.1 | loop fusion | flops 22013952 | bytes 12857344 | tf_op jit(solution)/shard_map/cond/branch_1_fun/while/body/eval_jaxpr/reduce_sum | solution.py:55
  178.2 1.4 fusion.46
  179.6 6.7 %fusion.47 = f32[2,8,384,128]{3,2,1,0:T(8,128)S(1)} fusion(f32[2,8,384,128]{3,2,1,0:T(8,128)S(1)} %copy-done, bf16[512,2,128,1]{0,2,3,1:T(8,128)(2,1)S(1)} %bitcast.72, f32[2,512,384,8]{2,1,3,0:T(8,128)S(1)} %get-tuple-element.512, f32[2,512]{1,0:T(2,128)S(1)} %get-tuple-element.515, f32[2,8,384]{2,1,0:T(8,128)S(1)} %select_maximum_fusion.2, ...), kind=kOutput, calls=%fused_computation.11.clone.1 | convolution fusion | flops 832831488 | bytes 19415040 | tf_op jit(solution)/shard_map/cond/branch_1_fun/while/body/eval_jaxpr/kgrn,nkd->kgrd/dot_general | solution.py:56
  186.4 1.6 copy-done.1
  188.0 2.4 copy.28
  190.3 0.7 compare_select_fusion
  191.1 0.3 divide_convert_fusion
  191.4 21.4 %convolution_convert_fusion = bf16[384,8192]{1,0:T(8,128)(2,1)} fusion(bf16[384,2048]{0,1:T(8,128)(2,1)S(1)} %bitcast.75, bf16[2048,8192]{1,0:T(8,128)(2,1)} %param.20), kind=kOutput, calls=%fused_computation.38 | convolution fusion | flops 12888047616 | bytes 41418752 | tf_op jit(solution)/shard_map/dot_general | solution.py:138
  212.9 111.8 %reduce-scatter.2.cloned.1.call-done = bf16[384,2048]{1,0:T(8,128)(2,1)} async-done(((bf16[384,8192]{1,0:T(8,128)(2,1)}), bf16[384,2048]{1,0:T(8,128)(2,1)}) %reduce-scatter.2.cloned.1.call-update) | async-done | bytes 1572880 | tf_op jit(solution)/shard_map/reduce_scatter | solution.py:139
  324.7 2.9 multiply_convert_fusion.4
  (52 shorter events, 0.3 us)
Async XLA Ops:
  6.5 28.9 %all-gather.3.cloned.1.call-start = ((), (), s32[]{:S(2)}) async-start(), calls=%async_computation.1 | async-start | bytes 1769472 | tf_op jit(solution)/shard_map/all_gather | solution.py:119
  8.3 54.9 %all-gather.5.cloned.1.call-start = ((), (), s32[]{:S(2)}) async-start(), calls=%async_computation.2 | async-start | bytes 1769472 | tf_op jit(solution)/shard_map/all_gather | solution.py:121
  10.1 314.6 %reduce-scatter.2.cloned.1.call-start = ((), (), s32[]{:S(2)}) async-start(), calls=%async_computation.3 | async-start | bytes 7864320 | tf_op jit(solution)/shard_map/reduce_scatter | solution.py:139
  73.2 4.7 %copy-start = (f32[2,8,384,128]{3,2,1,0:T(8,128)S(1)}, f32[2,8,384,128]{3,2,1,0:T(8,128)}, u32[]{:S(2)}) copy-start(f32[2,8,384,128]{3,2,1,0:T(8,128)} %get-tuple-element.536) | copy-start | bytes 9437188 | tf_op jit(solution)/shard_map/cond/branch_1_fun/while
  84.7 1.6 copy-start.1
  92.8 5.5 %copy-start = (f32[2,8,384,128]{3,2,1,0:T(8,128)S(1)}, f32[2,8,384,128]{3,2,1,0:T(8,128)}, u32[]{:S(2)}) copy-start(f32[2,8,384,128]{3,2,1,0:T(8,128)} %get-tuple-element.536) | copy-start | bytes 9437188 | tf_op jit(solution)/shard_map/cond/branch_1_fun/while
  105.0 1.6 copy-start.1
  113.1 5.5 %copy-start = (f32[2,8,384,128]{3,2,1,0:T(8,128)S(1)}, f32[2,8,384,128]{3,2,1,0:T(8,128)}, u32[]{:S(2)}) copy-start(f32[2,8,384,128]{3,2,1,0:T(8,128)} %get-tuple-element.536) | copy-start | bytes 9437188 | tf_op jit(solution)/shard_map/cond/branch_1_fun/while
  125.3 1.6 copy-start.1
  133.5 5.5 %copy-start = (f32[2,8,384,128]{3,2,1,0:T(8,128)S(1)}, f32[2,8,384,128]{3,2,1,0:T(8,128)}, u32[]{:S(2)}) copy-start(f32[2,8,384,128]{3,2,1,0:T(8,128)} %get-tuple-element.536) | copy-start | bytes 9437188 | tf_op jit(solution)/shard_map/cond/branch_1_fun/while
  145.7 1.6 copy-start.1
  153.8 5.5 %copy-start = (f32[2,8,384,128]{3,2,1,0:T(8,128)S(1)}, f32[2,8,384,128]{3,2,1,0:T(8,128)}, u32[]{:S(2)}) copy-start(f32[2,8,384,128]{3,2,1,0:T(8,128)} %get-tuple-element.536) | copy-start | bytes 9437188 | tf_op jit(solution)/shard_map/cond/branch_1_fun/while
  166.0 1.6 copy-start.1
  174.1 5.5 %copy-start = (f32[2,8,384,128]{3,2,1,0:T(8,128)S(1)}, f32[2,8,384,128]{3,2,1,0:T(8,128)}, u32[]{:S(2)}) copy-start(f32[2,8,384,128]{3,2,1,0:T(8,128)} %get-tuple-element.536) | copy-start | bytes 9437188 | tf_op jit(solution)/shard_map/cond/branch_1_fun/while
  186.3 1.6 copy-start.1
  212.8 111.9 %copy-start.2 = (f32[2048]{0:T(1024)S(1)}, f32[2048]{0:T(1024)}, u32[]{:S(2)}) copy-start(f32[2048]{0:T(1024)} %param.21) | copy-start | bytes 24580
Sparse Core Ops, SparseCore 0:
  9.2 26.1 all-gather.2
  37.3 25.8 all-gather.4
  213.0 111.6 reduce-scatter.1
where the time goes:
time: 337 us; the launch traced here: 334 us
  waiting for transfers between devices  146 us (43%)
  matrix products  95 us (28%)
  other arithmetic  36.8 us (11%)
  local copies, waits for them, and re-layouts  25.5 us (8%)
  blocking collectives  16.8 us (5%)
  between operations  13.1 us (4%)
    reduce_scatter x1, waiting for transfers between devices, local(): lax.psum_scatter(projected.astype(jnp.bfloat16), 'head', scatter_dimensio...  112 us
    dot_general x6, matrix products, attend_block(): jnp.einsum('kgrn,nkd->kgrd', weights, vals3, preferred_element_type=jnp.f...  40.4 us
    dot_general x6, matrix products, attend_block(): jnp.einsum('rkgd,nkd->kgrn', q_rows, keys3, preferred_element_type=jnp.fl...  30.1 us
    all_gather x1, waiting for transfers between devices, run_attention(): lax.all_gather(values, 'ctx', axis=0, tiled=True)  27.8 us
    reduce_sum x6, other arithmetic, attend_block(): total = total * decay + jnp.sum(expo, axis=3)  24.5 us
    dot_general x1, matrix products, local(): jnp.dot(attended, out_weight, preferred_element_type=jnp.float32)  21.4 us
    while x30, local copies, waits for them, and re-layouts  9.69 us
    all_gather x1, blocking collectives, run_attention(): lax.all_gather(value_scale, 'ctx', axis=0, tiled=True)  8.78 us
  transfers between devices with their start and end apart: 3, of which 3 were waited for; matrix products, arithmetic and copies ran while one was open for 1% of the time, Pallas kernels for 0%

commit v1 on v0

v1 whole, which is shorter than its diff:
```python
import functools
import math

import jax
import jax.numpy as jnp
from jax import lax
from jax.experimental import pallas as pl
from jax.experimental.pallas import tpu as pltpu
from jax.sharding import PartitionSpec as P

HD = 128
GROUP = 8
BLK = 128
PAD_ROWS = 16
NEG_FILL = -1e30


def attend_kernel(
    per_rank, mask_ref, rank_ref, q_ref, qs_ref, k_ref, v_ref, ks_ref, o_ref, order, factor, top, accum
):
    block = rank_ref[0] * per_rank + pl.program_id(1)
    stride = per_rank * BLK + PAD_ROWS

    def note(j, count):
        @pl.when(mask_ref[block, j] == 1)
        def _():
            order[count] = j

        return count + jnp.where(mask_ref[block, j] == 1, 1, 0)

    count = lax.fori_loop(0, block, note, jnp.int32(0))
    order[count] = block
    order[count + 1] = block
    padded = lax.rem(count, 2) == 0
    pairs = count // 2 + 1

    scale = math.log2(math.e) / math.sqrt(HD)
    for h in range(GROUP):
        column = qs_ref[0, :, h : h + 1].astype(jnp.float32) * scale
        factor[h] = jnp.broadcast_to(column, (BLK, HD))
    top[...] = jnp.full_like(top, NEG_FILL)
    accum[...] = jnp.zeros_like(accum)

    def rows_of(j):
        return pl.ds(pl.multiple_of((j // per_rank) * stride + lax.rem(j, per_rank) * BLK, PAD_ROWS), BLK)

    def step(pair, last):
        a, b = order[2 * pair], order[2 * pair + 1]
        keys = jnp.concatenate([k_ref[rows_of(a), :], k_ref[rows_of(b), :]], axis=0)
        vals = jnp.concatenate([v_ref[rows_of(a), :], v_ref[rows_of(b), :]], axis=0)
        vals = jnp.concatenate([vals, jnp.ones_like(vals)], axis=1)
        lanes = [pl.ds(pl.multiple_of(j * BLK, BLK), BLK) for j in (a, b)]
        key_sc = jnp.concatenate([ks_ref[0, :, lanes[0]], ks_ref[0, :, lanes[1]]], axis=1)
        if last:
            row = lax.broadcasted_iota(jnp.int32, (BLK, 2 * BLK), 0)
            col = lax.broadcasted_iota(jnp.int32, (BLK, 2 * BLK), 1)
            first_ok = jnp.where(padded, 0, BLK)
            allowed = (col < first_ok) | ((col >= BLK) & (col - BLK <= row))
        for h in range(GROUP):
            raw = lax.dot_general(
                q_ref[:, h * HD : (h + 1) * HD],
                keys,
                (((1,), (1,)), ((), ())),
                preferred_element_type=jnp.float32,
            )
            x = raw * key_sc
            if last:
                x = jnp.where(allowed, x, NEG_FILL)
            old = top[h]
            new = jnp.maximum(old, jnp.max(x, axis=1, keepdims=True))
            fac = factor[h]
            decay = jnp.exp2((old - new) * fac)
            expo = jnp.exp2(
                (x - jnp.concatenate([new, new], axis=1)) * jnp.concatenate([fac, fac], axis=1)
            )
            top[h] = new
            accum[h] = accum[h] * jnp.concatenate([decay, decay], axis=1) + jnp.dot(
                expo.astype(jnp.bfloat16), vals, preferred_element_type=jnp.float32
            )

    @pl.loop(0, pairs - 1)
    def _(pair):
        step(pair, False)

    step(pairs - 1, True)
    for h in range(GROUP):
        o_ref[:, h * HD : (h + 1) * HD] = (accum[h, :, :HD] / accum[h, :, HD:]).astype(jnp.bfloat16)


def attend(queries, query_scale, packed, key_sc, block_mask, rank):
    rows, width = queries.shape
    kv_local = width // (GROUP * HD)
    per_rank = rows // BLK
    count = block_mask.shape[0]
    q_sc = jnp.transpose(query_scale.reshape(rows, kv_local, GROUP), (1, 0, 2))
    return pl.pallas_call(
        functools.partial(attend_kernel, per_rank),
        out_shape=jax.ShapeDtypeStruct((rows, width), jnp.bfloat16),
        grid_spec=pltpu.PrefetchScalarGridSpec(
            num_scalar_prefetch=2,
            grid=(kv_local, per_rank),
            in_specs=[
                pl.BlockSpec((BLK, GROUP * HD), lambda g, i, *_: (i, g)),
                pl.BlockSpec((1, BLK, GROUP), lambda g, i, *_: (g, i, 0)),
                pl.BlockSpec((packed.shape[0], HD), lambda g, i, *_: (0, g)),
                pl.BlockSpec((packed.shape[0], HD), lambda g, i, *_: (0, kv_local + g)),
                pl.BlockSpec((1, 1, count * BLK), lambda g, i, *_: (g, 0, 0)),
            ],
            out_specs=pl.BlockSpec((BLK, GROUP * HD), lambda g, i, *_: (i, g)),
            scratch_shapes=[
                pltpu.SMEM((count + 2,), jnp.int32),
                pltpu.VMEM((GROUP, BLK, HD), jnp.float32),
                pltpu.VMEM((GROUP, BLK, HD), jnp.float32),
                pltpu.VMEM((GROUP, BLK, 2 * HD), jnp.float32),
            ],
        ),
        compiler_params=pltpu.CompilerParams(vmem_limit_bytes=24 * 2**20),
    )(block_mask, rank.reshape(1), queries, q_sc, packed, packed, key_sc)


def local(
    queries, query_scale, keys, key_scale, values, value_scale, block_mask, out_weight, out_scale
):
    rows = queries.shape[0]
    kv_local = keys.shape[1] // HD
    rank = lax.axis_index("ctx").astype(jnp.int32)
    scaled = (
        values.reshape(rows, kv_local, HD).astype(jnp.float32)
        * value_scale.astype(jnp.float32)[..., None]
    ).astype(jnp.bfloat16).reshape(rows, kv_local * HD)
    width = 2 * kv_local * HD
    slots = kv_local * (rows // BLK)
    tail = jnp.pad(key_scale.T.reshape(slots, BLK), ((0, PAD_ROWS - slots), (0, width - BLK)))
    packed = jnp.concatenate([jnp.concatenate([keys, scaled], axis=1), tail], axis=0)
    gathered = lax.all_gather(packed, "ctx", axis=0, tiled=True)
    ranks = gathered.shape[0] // packed.shape[0]
    key_sc = gathered.reshape(ranks, rows + PAD_ROWS, width)[:, rows : rows + slots, :BLK]
    key_sc = jnp.transpose(key_sc.astype(jnp.float32).reshape(ranks, kv_local, rows), (1, 0, 2))
    key_sc = key_sc.reshape(kv_local, 1, ranks * rows)
    attended = attend(queries, query_scale, gathered, key_sc, block_mask, rank)
    projected = jnp.dot(attended, out_weight, preferred_element_type=jnp.float32)
    summed = lax.psum_scatter(
        projected.astype(jnp.bfloat16), "head", scatter_dimension=1, tiled=True
    ).astype(jnp.float32)
    return (summed * out_scale[None, :]).astype(jnp.bfloat16)


def solution(mesh):
    return jax.shard_map(
        local,
        mesh=mesh,
        in_specs=(
            P("ctx", "head"),
            P("ctx", "head"),
            P("ctx", "head"),
            P("ctx", "head"),
            P("ctx", "head"),
            P("ctx", "head"),
            P(),
            P("head", None),
            P("head"),
        ),
        out_specs=P("ctx", "head"),
        check_vma=False,
    )
```

time: 337 us -> 220 us (0.65)
  matrix products: 95 us -> 20.8 us
  other arithmetic: 36.8 us -> 6.36 us
  Pallas kernels: 0 us -> 24.7 us
  local copies, waits for them, and re-layouts: 25.5 us -> 4.97 us
  blocking collectives: 16.8 us -> 0 us
    dot_general x19 -> x0, matrix products: 73.6 us -> none  [the longest x6 40.4 us: attend_block(): jnp.einsum('kgrn,nkd->kgrd', weights, vals3, preferred_element_type=jnp.f...]
    pallas_call x0 -> x1, Pallas kernels: none -> 24.7 us  [attend(): pl.pallas_call(functools.partial(attend_kernel, per_rank), out_shape=jax....]
    reduce_sum x6 -> x0, other arithmetic: 24.5 us -> none  [attend_block(): total = total * decay + jnp.sum(expo, axis=3)]
    all_gather x2 -> x0, blocking collectives: 16.8 us -> none  [the longest x1 8.78 us: run_attention(): lax.all_gather(value_scale, 'ctx', axis=0, tiled=True)]
    while x30 -> x0, local copies, waits for them, and re-layouts: 9.69 us -> none
    add x7 -> x0, other arithmetic: 7.44 us -> none  [the longest x6 7.43 us: attend_block(): total = total * decay + jnp.sum(expo, axis=3)]
    dynamic_slice x6 -> x0, local copies, waits for them, and re-layouts: 6.44 us -> none  [inner(): lax.dynamic_slice_in_dim(value_rows, offset, span, 0)]
    reduce_scatter x1, waiting for transfers between devices: 112 us -> 116 us  [local(): lax.psum_scatter(projected.astype(jnp.bfloat16), 'head', scatter_dimensio...]
  transfers between devices with their start and end apart: 3 -> 2, of which waited for: 3 -> 2; matrix products, arithmetic and copies ran while one was open for 1% -> 0% of each run, Pallas kernels for 0% -> 0%
where the time goes in v1:
time: 220 us; the launch traced here: 219 us
  waiting for transfers between devices  148 us (67%)
  Pallas kernels  24.7 us (11%)
  matrix products  20.8 us (9%)
  between operations  13.5 us (6%)
  other arithmetic  6.36 us (3%)
  local copies, waits for them, and re-layouts  4.97 us (2%)
    reduce_scatter x1, waiting for transfers between devices, local(): lax.psum_scatter(projected.astype(jnp.bfloat16), 'head', scatter_dimensio...  116 us
    all_gather x1, waiting for transfers between devices, local(): gathered = lax.all_gather(packed, 'ctx', axis=0, tiled=True)  32.3 us
    pallas_call x1, Pallas kernels, attend(): pl.pallas_call(functools.partial(attend_kernel, per_rank), out_shape=jax....  24.7 us
    dot_general x1, matrix products, local(): jnp.dot(attended, out_weight, preferred_element_type=jnp.float32)  20.8 us
  transfers between devices with their start and end apart: 2, of which 2 were waited for; matrix products, arithmetic and copies ran while one was open for 0% of the time, Pallas kernels for 0%

profile of v1, /device:TPU:6, one launch (start us, length us, event | category | flops | bytes accessed | tf_op | source)
XLA Modules:
  0.0 218.6 jit_solution(5550862837096138955)
XLA Ops:
  6.5 0.0 copy-start.2
  6.5 0.0 copy-start.1
  6.5 0.0 all-gather.2.cloned.1.call-start
  6.5 0.8 reshape.28
  7.4 0.8 copy.12
  8.2 0.5 mul.19
  8.7 1.0 fusion.2
  9.6 1.7 fusion.1
  11.4 0.0 all-gather.2.cloned.1.call-update
  11.4 0.0 reduce-scatter.2.cloned.1.call-start
  11.4 0.9 copy.11
  12.3 32.3 %all-gather.2.cloned.1.call-done.k_ref.v_ref = bf16[3200,512]{1,0:T(8,128)(2,1)} async-done(((bf16[400,512]{1,0:T(8,128)(2,1)}), bf16[3200,512]{1,0:T(8,128)(2,1)}) %all-gather.2.cloned.1.call-update) | async-done | bytes 3276816 | tf_op jit(solution)/shard_map/all_gather | solution.py:135
  44.7 0.7 slice_convert_fusion
  45.5 0.0 copy-done.2
  45.5 0.0 copy-done.1
  45.5 0.0 copy-start
  45.5 1.9 copy-done
  47.4 24.7 %shard_map.91 = bf16[384,2048]{1,0:T(8,128)(2,1)S(1)} custom-call(s32[24,24]{1,0:T(8,128)S(1)} %copy-done.2, s32[1]{0:T(128)} %bitcast.rank_ref, bf16[384,2048]{1,0:T(8,128)(2,1)S(1)} %copy-done.1, bf16[2,384,8]{2,1,0:T(8,128)(2,1)S(1)} %bitcast.14, bf16[3200,512]{1,0:T(8,128)(2,1)S(1)} %copy-done, bf16[3200,512]{1,0:T(8,128)(2,1)S(1)} %copy-done, ...), custom_call_target="tpu_custom_call" | custom-call | tf_op jit(solution)/shard_map/pallas_call | solution.py:96
  72.1 20.8 %convolution_convert_fusion = bf16[384,8192]{1,0:T(8,128)(2,1)} fusion(bf16[384,2048]{1,0:T(8,128)(2,1)S(1)} %shard_map.91, bf16[2048,8192]{1,0:T(8,128)(2,1)} %param.16), kind=kOutput, calls=%fused_computation | convolution fusion | flops 12888047616 | bytes 41418752 | tf_op jit(solution)/shard_map/dot_general | solution.py:141
  92.8 0.0 copy-start.3
  92.8 0.0 reduce-scatter.2.cloned.1.call-update
  92.8 116.0 %reduce-scatter.2.cloned.1.call-done = bf16[384,2048]{1,0:T(8,128)(2,1)} async-done(((bf16[384,8192]{1,0:T(8,128)(2,1)}), bf16[384,2048]{1,0:T(8,128)(2,1)}) %reduce-scatter.2.cloned.1.call-update) | async-done | bytes 1572880 | tf_op jit(solution)/shard_map/reduce_scatter | solution.py:142
  208.9 0.0 copy-done.3
  208.9 2.9 %multiply_convert_fusion = bf16[384,2048]{1,0:T(8,128)(2,1)} fusion(bf16[384,2048]{1,0:T(8,128)(2,1)} %reduce-scatter.2.cloned.1.call-done, f32[2048]{0:T(1024)S(1)} %copy-done.3), kind=kLoop, calls=%fused_computation.1 | loop fusion | flops 2359296 | bytes 3153920 | tf_op jit(solution)/shard_map/convert_element_type | solution.py:145
  (3 shorter events, 0.0 us)
Async XLA Ops:
  6.5 38.9 %copy-start.2 = (s32[24,24]{1,0:T(8,128)S(1)}, s32[24,24]{1,0:T(8,128)}, u32[]{:S(2)}) copy-start(s32[24,24]{1,0:T(8,128)} %mask_ref.1) | copy-start | bytes 6916
  6.5 38.9 %copy-start.1 = (bf16[384,2048]{1,0:T(8,128)(2,1)S(1)}, bf16[384,2048]{1,0:T(8,128)(2,1)}, u32[]{:S(2)}) copy-start(bf16[384,2048]{1,0:T(8,128)(2,1)} %q_ref.1) | copy-start | bytes 4718596
  6.5 38.1 %all-gather.2.cloned.1.call-start = ((), (), s32[]{:S(2)}) async-start(), calls=%async_computation.1 | async-start | bytes 3686400 | tf_op jit(solution)/shard_map/all_gather | solution.py:135
  11.4 197.5 %reduce-scatter.2.cloned.1.call-start = ((), (), s32[]{:S(2)}) async-start(), calls=%async_computation.2 | async-start | bytes 7864320 | tf_op jit(solution)/shard_map/reduce_scatter | solution.py:142
  45.5 1.9 copy-start
  92.8 116.1 %copy-start.3 = (f32[2048]{0:T(1024)S(1)}, f32[2048]{0:T(1024)}, u32[]{:S(2)}) copy-start(f32[2048]{0:T(1024)} %param.17) | copy-start | bytes 24580
Sparse Core Ops, SparseCore 0:
  11.5 33.1 all-gather.1
  93.0 115.8 reduce-scatter.1

commit v2 on v1

--- a/solution.py
+++ b/solution.py
@@ -87,18 +87,17 @@
         o_ref[:, h * HD : (h + 1) * HD] = (accum[h, :, :HD] / accum[h, :, HD:]).astype(jnp.bfloat16)
 
 
-def attend(queries, query_scale, packed, key_sc, block_mask, rank):
+def attend(queries, q_sc, packed, key_sc, block_mask, rank, blocks):
     rows, width = queries.shape
     kv_local = width // (GROUP * HD)
     per_rank = rows // BLK
     count = block_mask.shape[0]
-    q_sc = jnp.transpose(query_scale.reshape(rows, kv_local, GROUP), (1, 0, 2))
     return pl.pallas_call(
         functools.partial(attend_kernel, per_rank),
-        out_shape=jax.ShapeDtypeStruct((rows, width), jnp.bfloat16),
+        out_shape=jax.ShapeDtypeStruct((blocks * BLK, width), jnp.bfloat16),
         grid_spec=pltpu.PrefetchScalarGridSpec(
             num_scalar_prefetch=2,
-            grid=(kv_local, per_rank),
+            grid=(kv_local, blocks),
             in_specs=[
                 pl.BlockSpec((BLK, GROUP * HD), lambda g, i, *_: (i, g)),
                 pl.BlockSpec((1, BLK, GROUP), lambda g, i, *_: (g, i, 0)),
@@ -116,6 +115,290 @@
         ),
         compiler_params=pltpu.CompilerParams(vmem_limit_bytes=24 * 2**20),
     )(block_mask, rank.reshape(1), queries, q_sc, packed, packed, key_sc)
+
+
+def project_kernel(
+    n,
+    ranks,
+    first_ref,
+    q_ref,
+    qs_ref,
+    kv_ref,
+    ks_ref,
+    mask_ref,
+    w_hbm,
+    scale_ref,
+    o_ref,
+    weight,
+    attended,
+    parts,
+    factor,
+    top,
+    accum,
+    w_sem,
+    send_sem,
+    recv_sem,
+):
+    me = lax.axis_index("head")
+    rank = lax.axis_index("ctx")
+    chunks = attended.shape[0]
+    done = first_ref.shape[0] // BLK
+    kv_local = qs_ref.shape[0]
+    stride = chunks * BLK + PAD_ROWS
+    features = weight.shape[2]
+    tile = math.gcd(features, 512)
+    is_end = (me == 0) | (me == n - 1)
+
+    def load_weight(d):
+        return pltpu.make_async_copy(
+            w_hbm.at[:, pl.ds(pl.multiple_of(d * features, features), features)],
+            weight.at[d],
+            w_sem.at[d],
+        )
+
+    for s in range(n):
+        d = jnp.where(me < (n + 1) // 2, n - 1 - s, s)
+        load_weight(d).start()
+
+    barrier = pltpu.get_barrier_semaphore()
+
+    @pl.when(me > 0)
+    def _():
+        pl.semaphore_signal(
+            barrier, inc=1, device_id={"head": me - 1}, device_id_type=pl.DeviceIdType.MESH
+        )
+
+    @pl.when(me < n - 1)
+    def _():
+        pl.semaphore_signal(
+            barrier, inc=1, device_id={"head": me + 1}, device_id_type=pl.DeviceIdType.MESH
+        )
+
+    @pl.when(is_end)
+    def _():
+        pl.semaphore_wait(barrier, 1)
+
+    @pl.when(jnp.logical_not(is_end))
+    def _():
+        pl.semaphore_wait(barrier, 2)
+
+    for c in range(done):
+        attended[c] = first_ref[c * BLK : (c + 1) * BLK, :]
+
+    def attend_chunk(t):
+        block = rank * chunks + t
+        q_rows = pl.ds(pl.multiple_of(t * BLK, BLK), BLK)
+        scale = math.log2(math.e) / math.sqrt(HD)
+
+        @pl.loop(0, kv_local)
+        def _(g):
+            for h in range(GROUP):
+                column = qs_ref[g, q_rows, h : h + 1].astype(jnp.float32) * scale
+                factor[h] = jnp.broadcast_to(column, (BLK, HD))
+            top[...] = jnp.full_like(top, NEG_FILL)
+            accum[...] = jnp.zeros_like(accum)
+
+            @pl.loop(0, block // 2 + 1)
+            def _(pair):
+                a = 2 * pair
+                b = jnp.minimum(a + 1, ranks * chunks - 1)
+
+                def piece(j, column):
+                    begin = (j // chunks) * stride + lax.rem(j, chunks) * BLK
+                    return kv_ref[
+                        pl.ds(pl.multiple_of(begin, PAD_ROWS), BLK),
+                        pl.ds(pl.multiple_of(column * HD, HD), HD),
+                    ]
+
+                def lanes(j):
+                    return pl.ds(pl.multiple_of(j * BLK, BLK), BLK)
+
+                keys = jnp.concatenate([piece(a, g), piece(b, g)], axis=0)
+                vals = jnp.concatenate([piece(a, kv_local + g), piece(b, kv_local + g)], axis=0)
+                vals = jnp.concatenate([vals, jnp.ones_like(vals)], axis=1)
+                key_sc = jnp.concatenate([ks_ref[g, :, lanes(a)], ks_ref[g, :, lanes(b)]], axis=1)
+                read = jnp.concatenate([mask_ref[t, :, lanes(a)], mask_ref[t, :, lanes(b)]], axis=1)
+                row = lax.broadcasted_iota(jnp.int32, (BLK, 2 * BLK), 0) + block * BLK
+                col = lax.broadcasted_iota(jnp.int32, (BLK, 2 * BLK), 1) + a * BLK
+                allowed = (jnp.broadcast_to(read, (BLK, 2 * BLK)) == 1) & (col <= row)
+                for h in range(GROUP):
+                    column = pl.multiple_of((g * GROUP + h) * HD, HD)
+                    raw = lax.dot_general(
+                        q_ref[q_rows, pl.ds(column, HD)],
+                        keys,
+                        (((1,), (1,)), ((), ())),
+                        preferred_element_type=jnp.float32,
+                    )
+                    x = jnp.where(allowed, raw * key_sc, NEG_FILL)
+                    old = top[h]
+                    new = jnp.maximum(old, jnp.max(x, axis=1, keepdims=True))
+                    fac = factor[h]
+                    decay = jnp.exp2((old - new) * fac)
+                    expo = jnp.exp2(
+                        (x - jnp.concatenate([new, new], axis=1))
+                        * jnp.concatenate([fac, fac], axis=1)
+                    )
+                    top[h] = new
+                    accum[h] = accum[h] * jnp.concatenate([decay, decay], axis=1) + jnp.dot(
+                        expo.astype(jnp.bfloat16), vals, preferred_element_type=jnp.float32
+                    )
+
+            for h in range(GROUP):
+                column = pl.multiple_of((g * GROUP + h) * HD, HD)
+                attended[t, :, pl.ds(column, HD)] = (
+                    accum[h, :, :HD] / accum[h, :, HD:]
+                ).astype(jnp.bfloat16)
+
+    def products(c, d, use):
+        @pl.loop(0, features // tile)
+        def _(i):
+            cols = pl.ds(pl.multiple_of(i * tile, tile), tile)
+            use(
+                cols,
+                jnp.dot(attended[c], weight[d, :, cols], preferred_element_type=jnp.float32),
+            )
+
+    def hop(c, d, up):
+        slot = d if up else jnp.where(d == me - 1, n, d)
+        return pltpu.make_async_remote_copy(
+            src_ref=parts.at[c, d],
+            dst_ref=parts.at[c, slot],
+            send_sem=send_sem.at[c, d],
+            recv_sem=recv_sem.at[c, slot],
+            device_id={"head": me + 1 if up else me - 1},
+            device_id_type=pl.DeviceIdType.MESH,
+        )
+
+    def arrived(c, slot):
+        pltpu.make_async_copy(parts.at[c, slot], parts.at[c, slot], recv_sem.at[c, slot]).wait()
+
+    def relay(c, d, up):
+        source = me > 0 if up else me < n - 1
+
+        @pl.when(c == 0)
+        def _():
+            load_weight(d).wait()
+
+        @pl.when(source)
+        def _():
+            arrived(c, d)
+
+            def use(cols, product):
+                parts[c, d, :, cols] = (parts[c, d, :, cols].astype(jnp.float32) + product).astype(
+                    jnp.bfloat16
+                )
+
+            products(c, d, use)
+
+        @pl.when(jnp.logical_not(source))
+        def _():
+            def use(cols, product):
+                parts[c, d, :, cols] = product.astype(jnp.bfloat16)
+
+            products(c, d, use)
+
+        hop(c, d, up).start()
+
+    def forward(c):
+        @pl.loop(0, n - 1)
+        def _(s):
+            @pl.when(n - 1 - s > me)
+            def _():
+                relay(c, n - 1 - s, True)
+
+            @pl.when(s < me)
+            def _():
+                relay(c, s, False)
+
+    @pl.loop(0, chunks)
+    def _(t):
+        @pl.when(t >= done)
+        def _():
+            attend_chunk(t)
+
+        @pl.when(is_end)
+        def _():
+            forward(t)
+
+        @pl.when(jnp.logical_not(is_end) & (t > 0))
+        def _():
+            forward(t - 1)
+
+    @pl.when(jnp.logical_not(is_end))
+    def _():
+        forward(chunks - 1)
+
+    load_weight(me).wait()
+
+    @pl.loop(0, chunks)
+    def _(c):
+        rows = pl.ds(pl.multiple_of(c * BLK, BLK), BLK)
+
+        def finish(below, above):
+            if below:
+                arrived(c, me)
+            if above:
+                arrived(c, n)
+
+            def use(cols, product):
+                if below:
+                    product = product + parts[c, me, :, cols].astype(jnp.float32)
+                if above:
+                    product = product + parts[c, n, :, cols].astype(jnp.float32)
+                o_ref[rows, cols] = (product * scale_ref[:, cols]).astype(jnp.bfloat16)
+
+            products(c, me, use)
+
+        @pl.when(me == 0)
+        def _():
+            finish(False, True)
+
+        @pl.when(me == n - 1)
+        def _():
+            finish(True, False)
+
+        @pl.when(jnp.logical_not(is_end))
+        def _():
+            finish(True, True)
+
+        for d in range(n):
+
+            @pl.when(d > me)
+            def _():
+                hop(c, d, True).wait_send()
+
+            @pl.when(d < me)
+            def _():
+                hop(c, d, False).wait_send()
+
+
+def project(first, queries, q_sc, packed, key_sc, mask_rows, out_weight, out_scale):
+    n = lax.axis_size("head")
+    ranks = lax.axis_size("ctx")
+    rows, width = queries.shape
+    chunks = rows // BLK
+    features = out_weight.shape[1] // n
+    vmem = pl.BlockSpec(memory_space=pltpu.VMEM)
+    return pl.pallas_call(
+        functools.partial(project_kernel, n, ranks),
+        out_shape=jax.ShapeDtypeStruct((rows, features), jnp.bfloat16),
+        in_specs=[vmem] * 6 + [pl.BlockSpec(memory_space=pl.ANY), vmem],
+        out_specs=vmem,
+        scratch_shapes=[
+            pltpu.VMEM((n, width, features), jnp.bfloat16),
+            pltpu.VMEM((chunks, BLK, width), jnp.bfloat16),
+            pltpu.VMEM((chunks, n + 1, BLK, features), jnp.bfloat16),
+            pltpu.VMEM((GROUP, BLK, HD), jnp.float32),
+            pltpu.VMEM((GROUP, BLK, HD), jnp.float32),
+            pltpu.VMEM((GROUP, BLK, 2 * HD), jnp.float32),
+            pltpu.SemaphoreType.DMA((n,)),
+            pltpu.SemaphoreType.DMA((chunks, n)),
+            pltpu.SemaphoreType.DMA((chunks, n + 1)),
+        ],
+        compiler_params=pltpu.CompilerParams(
+            collective_id=0, has_side_effects=True, vmem_limit_bytes=60 * 2**20
+        ),
+    )(first, queries, q_sc, packed, key_sc, mask_rows, out_weight, out_scale.reshape(1, -1))
 
 
 def local(
@@ -137,12 +420,11 @@
     key_sc = gathered.reshape(ranks, rows + PAD_ROWS, width)[:, rows : rows + slots, :BLK]
     key_sc = jnp.transpose(key_sc.astype(jnp.float32).reshape(ranks, kv_local, rows), (1, 0, 2))
     key_sc = key_sc.reshape(kv_local, 1, ranks * rows)
-    attended = attend(queries, query_scale, gathered, key_sc, block_mask, rank)
-    projected = jnp.dot(attended, out_weight, preferred_element_type=jnp.float32)
-    summed = lax.psum_scatter(
-        projected.astype(jnp.bfloat16), "head", scatter_dimension=1, tiled=True
-    ).astype(jnp.float32)
-    return (summed * out_scale[None, :]).astype(jnp.bfloat16)
+    q_sc = jnp.transpose(query_scale.reshape(rows, kv_local, GROUP), (1, 0, 2))
+    own = lax.dynamic_slice_in_dim(block_mask, rank * (rows // BLK), rows // BLK, 0)
+    mask_rows = jnp.repeat(own, BLK, axis=1)[:, None, :]
+    first = attend(queries, q_sc, gathered, key_sc, block_mask, rank, 1)
+    return project(first, queries, q_sc, gathered, key_sc, mask_rows, out_weight, out_scale)
 
 
 def solution(mesh):

time: 220 us -> 238 us (1.082)
  Pallas kernels: 24.7 us -> 178 us
  waiting for transfers between devices: 148 us -> 31.7 us
  matrix products: 20.8 us -> 0 us
  local copies, waits for them, and re-layouts: 4.97 us -> 10.6 us
  other arithmetic: 6.36 us -> 3.41 us
    pallas_call x0 -> x1, Pallas kernels: none -> 167 us  [project(): pl.pallas_call(functools.partial(project_kernel, n, ranks), out_shape=jax...]
    reduce_scatter x1 -> x0, waiting for transfers between devices: 116 us -> none  [local(): lax.psum_scatter(projected.astype(jnp.bfloat16), 'head', scatter_dimensio...]
    dot_general x1 -> x0, matrix products: 20.8 us -> none  [local(): jnp.dot(attended, out_weight, preferred_element_type=jnp.float32)]
    pallas_call x1, Pallas kernels: 24.7 us -> 10.4 us  [attend(): pl.pallas_call(functools.partial(attend_kernel, per_rank), out_shape=jax....]
    unnamed x8 -> x13, local copies, waits for them, and re-layouts: 1.93 us -> 6.15 us
    convert_element_type x1 -> x0, other arithmetic: 2.94 us -> none  [local(): return (summed * out_scale[None, :]).astype(jnp.bfloat16)]
  transfers between devices with their start and end apart: 2 -> 1, of which waited for: 2 -> 1; matrix products, arithmetic and copies ran while one was open for 0% -> 1% of each run, Pallas kernels for 0% -> 0%
where the time goes in v2:
time: 238 us; the launch traced here: 237 us
  Pallas kernels  178 us (75%)
  waiting for transfers between devices  31.7 us (13%)
  between operations  13.5 us (6%)
  local copies, waits for them, and re-layouts  10.6 us (4%)
  other arithmetic  3.41 us (1%)
    pallas_call x1, Pallas kernels, project(): pl.pallas_call(functools.partial(project_kernel, n, ranks), out_shape=jax...  167 us
    all_gather x1, waiting for transfers between devices, local(): gathered = lax.all_gather(packed, 'ctx', axis=0, tiled=True)  31.6 us
    pallas_call x1, Pallas kernels, attend(): pl.pallas_call(functools.partial(attend_kernel, per_rank), out_shape=jax....  10.4 us
    unnamed x13, local copies, waits for them, and re-layouts  6.15 us
  transfers between devices with their start and end apart: 1, of which 1 were waited for; matrix products, arithmetic and copies ran while one was open for 1% of the time, Pallas kernels for 0%

profile of v2, /device:TPU:6, one launch (start us, length us, event | category | flops | bytes accessed | tf_op | source)
XLA Modules:
  0.0 237.0 jit_solution(1516555549152557630)
XLA Ops:
  6.5 0.0 copy-start.1
  6.5 0.0 all-gather.2.cloned.1.call-start
  6.5 0.8 reshape.30
  7.4 0.8 copy.12
  8.2 0.5 mul.14
  8.7 1.0 fusion.2
  9.6 1.7 fusion.1
  11.3 0.0 all-gather.2.cloned.1.call-update
  11.4 0.9 copy.11
  12.3 0.0 copy-start.3
  12.3 0.7 constant_dynamic-slice_fusion
  13.0 31.6 %all-gather.2.cloned.1.call-done.k_ref.v_ref.kv_ref = bf16[3200,512]{1,0:T(8,128)(2,1)} async-done(((bf16[400,512]{1,0:T(8,128)(2,1)}), bf16[3200,512]{1,0:T(8,128)(2,1)}) %all-gather.2.cloned.1.call-update) | async-done | bytes 3276816 | tf_op jit(solution)/shard_map/all_gather | solution.py:418
  44.6 0.7 slice_convert_fusion
  45.4 0.0 copy-start.4
  45.4 0.0 copy-done.1
  45.5 0.0 copy-start
  45.5 1.9 copy-done
  47.4 0.0 copy-start.5
  47.4 0.7 copy-done.5
  48.1 10.4 %shard_map.91.first_ref = bf16[128,2048]{1,0:T(8,128)(2,1)S(1)} custom-call(s32[24,24]{1,0:T(8,128)S(1)} %copy-done.5, s32[1]{0:T(128)} %bitcast.rank_ref, bf16[384,2048]{1,0:T(8,128)(2,1)S(1)} %copy-done.1, bf16[2,384,8]{2,1,0:T(8,128)(2,1)S(1)} %bitcast.14, bf16[3200,512]{1,0:T(8,128)(2,1)S(1)} %copy-done, bf16[3200,512]{1,0:T(8,128)(2,1)S(1)} %copy-done, ...), custom_call_target="tpu_custom_call" | custom-call | tf_op jit(solution)/shard_map/pallas_call | solution.py:95
  58.5 0.0 copy-done.3
  58.5 0.0 copy-done.4
  58.5 0.0 copy-start.2
  58.5 0.8 copy-done.2
  59.3 0.7 broadcast_in_dim.4
  60.0 167.5 %shard_map.92 = bf16[384,2048]{1,0:T(8,128)(2,1)} custom-call(bf16[128,2048]{1,0:T(8,128)(2,1)} %copy-done.2, bf16[384,2048]{1,0:T(8,128)(2,1)} %q_ref.3, bf16[2,384,8]{2,1,0:T(8,128)(2,1)} %bitcast.15, bf16[3200,512]{1,0:T(8,128)(2,1)} %all-gather.2.cloned.1.call-done.k_ref.v_ref.kv_ref, f32[2,1,3072]{2,1,0:T(1,128)} %copy-done.4, s32[3,1,3072]{2,1,0:T(1,128)} %bitcast.17, ...), custom_call_target="tpu_custom_call" | custom-call | tf_op jit(solution)/shard_map/pallas_call | solution.py:382
  227.5 2.7 %copy.17 = bf16[384,2048]{1,0:T(8,128)(2,1)} copy(bf16[384,2048]{1,0:T(8,128)(2,1)} %shard_map.92) | data formatting | bytes 3145728
  (3 shorter events, 0.0 us)
Async XLA Ops:
  6.5 38.9 %copy-start.1 = (bf16[384,2048]{1,0:T(8,128)(2,1)S(1)}, bf16[384,2048]{1,0:T(8,128)(2,1)}, u32[]{:S(2)}) copy-start(bf16[384,2048]{1,0:T(8,128)(2,1)} %q_ref.3) | copy-start | bytes 4718596
  6.5 38.1 %all-gather.2.cloned.1.call-start = ((), (), s32[]{:S(2)}) async-start(), calls=%async_computation | async-start | bytes 3686400 | tf_op jit(solution)/shard_map/all_gather | solution.py:418
  12.3 46.2 %copy-start.3 = (bf16[384,2,8]{2,0,1:T(8,128)(2,1)}, bf16[384,2,8]{2,0,1:T(8,128)(2,1)S(1)}, u32[]{:S(2)}) copy-start(bf16[384,2,8]{2,0,1:T(8,128)(2,1)S(1)} %copy.11) | copy-start | bytes 36868
  45.4 13.1 %copy-start.4 = (f32[2,1,3072]{2,1,0:T(1,128)}, f32[2,1,3072]{2,1,0:T(1,128)S(1)}, u32[]{:S(2)}) copy-start(f32[2,1,3072]{2,1,0:T(1,128)S(1)} %reshape.37.ks_ref) | copy-start | bytes 73732
  45.5 1.9 copy-start
  47.4 0.7 copy-start.5
  58.5 0.8 copy-start.2
Sparse Core Ops, SparseCore 0:
  11.5 33.1 all-gather.1

commit v3 on v2

--- a/solution.py
+++ b/solution.py
@@ -12,6 +12,7 @@
 GROUP = 8
 BLK = 128
 PAD_ROWS = 16
+DEPTH = 2
 NEG_FILL = -1e30
 
 
@@ -272,7 +273,16 @@
     def arrived(c, slot):
         pltpu.make_async_copy(parts.at[c, slot], parts.at[c, slot], recv_sem.at[c, slot]).wait()
 
-    def relay(c, d, up):
+    def count_of(up):
+        return n - 1 - me if up else me
+
+    def nth(q, up):
+        per = jnp.maximum(count_of(up), 1)
+        k = lax.rem(q, per)
+        return hop(lax.div(q, per), n - 1 - k if up else k, up)
+
+    def relay(c, k, up):
+        d = n - 1 - k if up else k
         source = me > 0 if up else me < n - 1
 
         @pl.when(c == 0)
@@ -297,18 +307,34 @@
 
             products(c, d, use)
 
-        hop(c, d, up).start()
+        q = c * count_of(up) + k
+
+        @pl.when(q >= DEPTH)
+        def _():
+            nth(q - DEPTH, up).wait_send()
+
+        nth(q, up).start()
 
     def forward(c):
-        @pl.loop(0, n - 1)
-        def _(s):
-            @pl.when(n - 1 - s > me)
-            def _():
-                relay(c, n - 1 - s, True)
-
-            @pl.when(s < me)
-            def _():
-                relay(c, s, False)
+        def ups():
+            @pl.loop(0, n - 1 - me)
+            def _(k):
+                relay(c, k, True)
+
+        def downs():
+            @pl.loop(0, me)
+            def _(k):
+                relay(c, k, False)
+
+        @pl.when(me < n // 2)
+        def _():
+            ups()
+            downs()
+
+        @pl.when(me >= n // 2)
+        def _():
+            downs()
+            ups()
 
     @pl.loop(0, chunks)
     def _(t):
@@ -361,15 +387,75 @@
         def _():
             finish(True, True)
 
-        for d in range(n):
-
-            @pl.when(d > me)
-            def _():
-                hop(c, d, True).wait_send()
-
-            @pl.when(d < me)
-            def _():
-                hop(c, d, False).wait_send()
+    for up in (True, False):
+        total = chunks * count_of(up)
+
+        @pl.loop(jnp.maximum(total - DEPTH, 0), total)
+        def _(q):
+            nth(q, up).wait_send()
+
+
+def gather_kernel(ranks, x_ref, o_ref, own_sem, send_sem, pass_sem, recv_sem):
+    rank = lax.axis_index("ctx")
+    chips = ranks // 2
+    other = rank + 1 - 2 * lax.rem(rank, 2)
+
+    def send(src, slot, sem, target):
+        return pltpu.make_async_remote_copy(
+            src_ref=src,
+            dst_ref=o_ref.at[slot],
+            send_sem=sem,
+            recv_sem=recv_sem.at[slot],
+            device_id={"ctx": target},
+            device_id_type=pl.DeviceIdType.MESH,
+        )
+
+    def arrived(slot):
+        pltpu.make_async_copy(o_ref.at[slot], o_ref.at[slot], recv_sem.at[slot]).wait()
+
+    own = pltpu.make_async_copy(x_ref, o_ref.at[rank], own_sem)
+    own.start()
+    barrier = pltpu.get_barrier_semaphore()
+    peers = [lax.rem(rank + 2 * j, ranks) for j in range(1, chips)]
+    for target in peers + [other]:
+        pl.semaphore_signal(
+            barrier, inc=1, device_id={"ctx": target}, device_id_type=pl.DeviceIdType.MESH
+        )
+    pl.semaphore_wait(barrier, chips)
+    sends = [send(x_ref, rank, send_sem.at[j], target) for j, target in enumerate(peers)]
+    sends.append(send(x_ref, rank, send_sem.at[chips - 1], other))
+    for copy in sends:
+        copy.start()
+    for j in range(1, chips):
+        slot = lax.rem(rank + 2 * j, ranks)
+        arrived(slot)
+        copy = send(o_ref.at[slot], slot, pass_sem.at[j], other)
+        copy.start()
+        sends.append(copy)
+    for j in range(chips):
+        arrived(lax.rem(other + 2 * j, ranks))
+    for copy in sends:
+        copy.wait_send()
+    own.wait()
+
+
+def gather(packed):
+    ranks = lax.axis_size("ctx")
+    chips = ranks // 2
+    out = pl.pallas_call(
+        functools.partial(gather_kernel, ranks),
+        out_shape=jax.ShapeDtypeStruct((ranks,) + packed.shape, packed.dtype),
+        in_specs=[pl.BlockSpec(memory_space=pl.ANY)],
+        out_specs=pl.BlockSpec(memory_space=pl.ANY),
+        scratch_shapes=[
+            pltpu.SemaphoreType.DMA,
+            pltpu.SemaphoreType.DMA((chips,)),
+            pltpu.SemaphoreType.DMA((chips,)),
+            pltpu.SemaphoreType.DMA((ranks,)),
+        ],
+        compiler_params=pltpu.CompilerParams(collective_id=1, has_side_effects=True),
+    )(packed)
+    return out.reshape(ranks * packed.shape[0], packed.shape[1])
 
 
 def project(first, queries, q_sc, packed, key_sc, mask_rows, out_weight, out_scale):
@@ -415,7 +501,7 @@
     slots = kv_local * (rows // BLK)
     tail = jnp.pad(key_scale.T.reshape(slots, BLK), ((0, PAD_ROWS - slots), (0, width - BLK)))
     packed = jnp.concatenate([jnp.concatenate([keys, scaled], axis=1), tail], axis=0)
-    gathered = lax.all_gather(packed, "ctx", axis=0, tiled=True)
+    gathered = gather(packed)
     ranks = gathered.shape[0] // packed.shape[0]
     key_sc = gathered.reshape(ranks, rows + PAD_ROWS, width)[:, rows : rows + slots, :BLK]
     key_sc = jnp.transpose(key_sc.astype(jnp.float32).reshape(ranks, kv_local, rows), (1, 0, 2))

time: 238 us -> 166 us (0.70)
  the two profiles are of different devices: /device:TPU:6 before, /device:TPU:0 now
where the time goes in v3:
time: 166 us; the launch traced here: 165 us
  Pallas kernels  152 us (92%)
  local copies, waits for them, and re-layouts  9.87 us (6%)
  other arithmetic  3.42 us (2%)
    pallas_call x1, Pallas kernels, project(): pl.pallas_call(functools.partial(project_kernel, n, ranks), out_shape=jax...  123 us
    pallas_call x1, Pallas kernels, gather(): pl.pallas_call(functools.partial(gather_kernel, ranks), out_shape=jax.Sha...  25.8 us
    unnamed x13, local copies, waits for them, and re-layouts  5.45 us
    pallas_call x1, Pallas kernels, attend(): pl.pallas_call(functools.partial(attend_kernel, per_rank), out_shape=jax....  3.34 us

profile of v3, /device:TPU:0, one launch (start us, length us, event | category | flops | bytes accessed | tf_op | source)
XLA Modules:
  0.0 165.3 jit_solution(7224331474997814624)
XLA Ops:
  0.0 0.0 copy-start.1
  0.0 0.0 copy-start.5
  0.0 0.8 constant_dynamic-slice_fusion
  0.8 0.7 reshape.30
  1.5 0.7 broadcast_in_dim.4
  2.2 0.9 copy.12
  3.1 0.0 copy-start.3
  3.1 0.8 copy.13
  3.9 0.5 mul.14
  4.4 1.0 fusion.2
  5.4 1.7 %fusion.1.x_ref = bf16[400,512]{1,0:T(8,128)(2,1)} fusion(bf16[6,128]{1,0:T(8,128)(2,1)S(1)} %reshape.30, bf16[384,256]{1,0:T(8,128)(2,1)S(1)} %fusion.2, bf16[384,256]{1,0:T(8,128)(2,1)} %param.11), kind=kLoop, calls=%fused_computation.2 | loop fusion | flops 1638400 | bytes 804352 | tf_op jit(solution)/shard_map/concatenate | solution.py:503
  7.1 25.8 %shard_map.91 = bf16[8,400,512]{2,1,0:T(8,128)(2,1)} custom-call(bf16[400,512]{1,0:T(8,128)(2,1)} %fusion.1.x_ref), custom_call_target="tpu_custom_call" | custom-call | tf_op jit(solution)/shard_map/pallas_call | solution.py:445
  32.9 0.7 slice_convert_fusion
  33.7 0.0 copy-done.1
  33.7 0.0 copy-done.5
  33.7 0.0 copy-start
  33.7 1.9 %copy-done = bf16[8,400,512]{2,1,0:T(8,128)(2,1)S(1)} copy-done((bf16[8,400,512]{2,1,0:T(8,128)(2,1)S(1)}, bf16[8,400,512]{2,1,0:T(8,128)(2,1)}, u32[]{:S(2)}) %copy-start) | copy-done | bytes 3276824
  35.6 0.0 copy-start.4
  35.6 3.3 %shard_map.92.first_ref = bf16[128,2048]{1,0:T(8,128)(2,1)S(1)} custom-call(s32[24,24]{1,0:T(8,128)S(1)} %copy-done.5, s32[1]{0:T(128)} %bitcast.rank_ref, bf16[384,2048]{1,0:T(8,128)(2,1)S(1)} %copy-done.1, bf16[2,384,8]{2,1,0:T(8,128)(2,1)S(1)} %bitcast.16, bf16[3200,512]{1,0:T(8,128)(2,1)S(1)} %bitcast.14, bf16[3200,512]{1,0:T(8,128)(2,1)S(1)} %bitcast.15, ...), custom_call_target="tpu_custom_call" | custom-call | tf_op jit(solution)/shard_map/pallas_call | solution.py:96
  39.0 0.0 copy-done.3
  39.0 0.0 copy-done.4
  39.0 0.0 copy-start.2
  39.0 0.8 copy-done.2
  39.8 122.8 %shard_map.93 = bf16[384,2048]{1,0:T(8,128)(2,1)} custom-call(bf16[128,2048]{1,0:T(8,128)(2,1)} %copy-done.2, bf16[384,2048]{1,0:T(8,128)(2,1)} %q_ref.3, bf16[2,384,8]{2,1,0:T(8,128)(2,1)} %bitcast.17, bf16[3200,512]{1,0:T(8,128)(2,1)} %bitcast.13, f32[2,1,3072]{2,1,0:T(1,128)} %copy-done.4, s32[3,1,3072]{2,1,0:T(1,128)} %bitcast.19, ...), custom_call_target="tpu_custom_call" | custom-call | tf_op jit(solution)/shard_map/pallas_call | solution.py:468
  162.6 2.7 %copy.18 = bf16[384,2048]{1,0:T(8,128)(2,1)} copy(bf16[384,2048]{1,0:T(8,128)(2,1)} %shard_map.93) | data formatting | bytes 3145728
  (3 shorter events, 0.0 us)
Async XLA Ops:
  0.0 33.7 %copy-start.1 = (bf16[384,2048]{1,0:T(8,128)(2,1)S(1)}, bf16[384,2048]{1,0:T(8,128)(2,1)}, u32[]{:S(2)}) copy-start(bf16[384,2048]{1,0:T(8,128)(2,1)} %q_ref.3) | copy-start | bytes 4718596
  0.0 33.7 %copy-start.5 = (s32[24,24]{1,0:T(8,128)S(1)}, s32[24,24]{1,0:T(8,128)}, u32[]{:S(2)}) copy-start(s32[24,24]{1,0:T(8,128)} %mask_ref.1) | copy-start | bytes 6916
  3.1 35.9 %copy-start.3 = (bf16[384,2,8]{2,0,1:T(8,128)(2,1)}, bf16[384,2,8]{2,0,1:T(8,128)(2,1)S(1)}, u32[]{:S(2)}) copy-start(bf16[384,2,8]{2,0,1:T(8,128)(2,1)S(1)} %copy.12) | copy-start | bytes 36868
  33.7 1.9 %copy-start = (bf16[8,400,512]{2,1,0:T(8,128)(2,1)S(1)}, bf16[8,400,512]{2,1,0:T(8,128)(2,1)}, u32[]{:S(2)}) copy-start(bf16[8,400,512]{2,1,0:T(8,128)(2,1)} %shard_map.91) | copy-start | bytes 9830404
  35.6 3.4 %copy-start.4 = (f32[2,1,3072]{2,1,0:T(1,128)}, f32[2,1,3072]{2,1,0:T(1,128)S(1)}, u32[]{:S(2)}) copy-start(f32[2,1,3072]{2,1,0:T(1,128)S(1)} %reshape.37.ks_ref) | copy-start | bytes 73732
  39.0 0.8 copy-start.2

commit v4 on v3

--- a/solution.py
+++ b/solution.py
@@ -12,7 +12,6 @@
 GROUP = 8
 BLK = 128
 PAD_ROWS = 16
-DEPTH = 2
 NEG_FILL = -1e30
 
 
@@ -157,9 +156,12 @@
             w_sem.at[d],
         )
 
-    for s in range(n):
-        d = jnp.where(me < (n + 1) // 2, n - 1 - s, s)
-        load_weight(d).start()
+    load_weight(jnp.where(me < (n + 1) // 2, n - 1, 0)).start()
+
+    @pl.when(jnp.logical_not(is_end))
+    def _():
+        for s in range(1, n):
+            load_weight(jnp.where(me < (n + 1) // 2, n - 1 - s, s)).start()
 
     barrier = pltpu.get_barrier_semaphore()
 
@@ -289,6 +291,10 @@
         def _():
             load_weight(d).wait()
 
+            @pl.when(is_end)
+            def _():
+                load_weight(d - 1 if up else d + 1).start()
+
         @pl.when(source)
         def _():
             arrived(c, d)
@@ -309,9 +315,15 @@
 
         q = c * count_of(up) + k
 
-        @pl.when(q >= DEPTH)
-        def _():
-            nth(q - DEPTH, up).wait_send()
+        final = c == chunks - 1
+
+        @pl.when((q >= 2) & (jnp.logical_not(final) | (k == 0)))
+        def _():
+            nth(q - 2, up).wait_send()
+
+        @pl.when((q >= 1) & final)
+        def _():
+            nth(q - 1, up).wait_send()
 
         nth(q, up).start()
 
@@ -390,9 +402,9 @@
     for up in (True, False):
         total = chunks * count_of(up)
 
-        @pl.loop(jnp.maximum(total - DEPTH, 0), total)
-        def _(q):
-            nth(q, up).wait_send()
+        @pl.when(total > 0)
+        def _():
+            nth(total - 1, up).wait_send()
 
 
 def gather_kernel(ranks, x_ref, o_ref, own_sem, send_sem, pass_sem, recv_sem):

time: 166 us -> 171 us (1.030)
  the two profiles are of different devices: /device:TPU:0 before, /device:TPU:6 now
where the time goes in v4:
time: 171 us; the launch traced here: 170 us
  Pallas kernels  157 us (92%)
  local copies, waits for them, and re-layouts  9.86 us (6%)
  other arithmetic  3.42 us (2%)
    pallas_call x1, Pallas kernels, project(): pl.pallas_call(functools.partial(project_kernel, n, ranks), out_shape=jax...  124 us
    pallas_call x1, Pallas kernels, gather(): pl.pallas_call(functools.partial(gather_kernel, ranks), out_shape=jax.Sha...  24.2 us
    pallas_call x1, Pallas kernels, attend(): pl.pallas_call(functools.partial(attend_kernel, per_rank), out_shape=jax....  9.07 us
    unnamed x13, local copies, waits for them, and re-layouts  5.45 us

profile of v4, /device:TPU:6, one launch (start us, length us, event | category | flops | bytes accessed | tf_op | source)
XLA Modules:
  0.0 170.4 jit_solution(401262165113158553)
XLA Ops:
  0.0 0.0 copy-start.1
  0.0 0.0 copy-start.5
  0.0 0.8 constant_dynamic-slice_fusion
  0.8 0.7 reshape.30
  1.5 0.7 broadcast_in_dim.4
  2.2 0.9 copy.12
  3.1 0.0 copy-start.3
  3.1 0.8 copy.13
  3.9 0.5 mul.14
  4.4 1.0 fusion.2
  5.4 1.7 %fusion.1.x_ref = bf16[400,512]{1,0:T(8,128)(2,1)} fusion(bf16[6,128]{1,0:T(8,128)(2,1)S(1)} %reshape.30, bf16[384,256]{1,0:T(8,128)(2,1)S(1)} %fusion.2, bf16[384,256]{1,0:T(8,128)(2,1)} %param.11), kind=kLoop, calls=%fused_computation.2 | loop fusion | flops 1638400 | bytes 804352 | tf_op jit(solution)/shard_map/concatenate | solution.py:515
  7.1 24.2 %shard_map.91 = bf16[8,400,512]{2,1,0:T(8,128)(2,1)} custom-call(bf16[400,512]{1,0:T(8,128)(2,1)} %fusion.1.x_ref), custom_call_target="tpu_custom_call" | custom-call | tf_op jit(solution)/shard_map/pallas_call | solution.py:457
  31.3 0.7 slice_convert_fusion
  32.1 0.0 copy-done.1
  32.1 0.0 copy-done.5
  32.1 0.0 copy-start
  32.2 1.9 %copy-done = bf16[8,400,512]{2,1,0:T(8,128)(2,1)S(1)} copy-done((bf16[8,400,512]{2,1,0:T(8,128)(2,1)S(1)}, bf16[8,400,512]{2,1,0:T(8,128)(2,1)}, u32[]{:S(2)}) %copy-start) | copy-done | bytes 3276824
  34.1 0.0 copy-start.4
  34.1 9.1 %shard_map.92.first_ref = bf16[128,2048]{1,0:T(8,128)(2,1)S(1)} custom-call(s32[24,24]{1,0:T(8,128)S(1)} %copy-done.5, s32[1]{0:T(128)} %bitcast.rank_ref, bf16[384,2048]{1,0:T(8,128)(2,1)S(1)} %copy-done.1, bf16[2,384,8]{2,1,0:T(8,128)(2,1)S(1)} %bitcast.16, bf16[3200,512]{1,0:T(8,128)(2,1)S(1)} %bitcast.14, bf16[3200,512]{1,0:T(8,128)(2,1)S(1)} %bitcast.15, ...), custom_call_target="tpu_custom_call" | custom-call | tf_op jit(solution)/shard_map/pallas_call | solution.py:95
  43.1 0.0 copy-done.3
  43.2 0.0 copy-done.4
  43.2 0.0 copy-start.2
  43.2 0.8 copy-done.2
  44.0 123.7 %shard_map.93 = bf16[384,2048]{1,0:T(8,128)(2,1)} custom-call(bf16[128,2048]{1,0:T(8,128)(2,1)} %copy-done.2, bf16[384,2048]{1,0:T(8,128)(2,1)} %q_ref.3, bf16[2,384,8]{2,1,0:T(8,128)(2,1)} %bitcast.17, bf16[3200,512]{1,0:T(8,128)(2,1)} %bitcast.13, f32[2,1,3072]{2,1,0:T(1,128)} %copy-done.4, s32[3,1,3072]{2,1,0:T(1,128)} %bitcast.19, ...), custom_call_target="tpu_custom_call" | custom-call | tf_op jit(solution)/shard_map/pallas_call | solution.py:480
  167.7 2.7 %copy.18 = bf16[384,2048]{1,0:T(8,128)(2,1)} copy(bf16[384,2048]{1,0:T(8,128)(2,1)} %shard_map.93) | data formatting | bytes 3145728
  (3 shorter events, 0.0 us)
Async XLA Ops:
  0.0 32.1 %copy-start.1 = (bf16[384,2048]{1,0:T(8,128)(2,1)S(1)}, bf16[384,2048]{1,0:T(8,128)(2,1)}, u32[]{:S(2)}) copy-start(bf16[384,2048]{1,0:T(8,128)(2,1)} %q_ref.3) | copy-start | bytes 4718596
  0.0 32.1 %copy-start.5 = (s32[24,24]{1,0:T(8,128)S(1)}, s32[24,24]{1,0:T(8,128)}, u32[]{:S(2)}) copy-start(s32[24,24]{1,0:T(8,128)} %mask_ref.1) | copy-start | bytes 6916
  3.1 40.1 %copy-start.3 = (bf16[384,2,8]{2,0,1:T(8,128)(2,1)}, bf16[384,2,8]{2,0,1:T(8,128)(2,1)S(1)}, u32[]{:S(2)}) copy-start(bf16[384,2,8]{2,0,1:T(8,128)(2,1)S(1)} %copy.12) | copy-start | bytes 36868
  32.1 1.9 %copy-start = (bf16[8,400,512]{2,1,0:T(8,128)(2,1)S(1)}, bf16[8,400,512]{2,1,0:T(8,128)(2,1)}, u32[]{:S(2)}) copy-start(bf16[8,400,512]{2,1,0:T(8,128)(2,1)} %shard_map.91) | copy-start | bytes 9830404
  34.1 9.1 %copy-start.4 = (f32[2,1,3072]{2,1,0:T(1,128)}, f32[2,1,3072]{2,1,0:T(1,128)S(1)}, u32[]{:S(2)}) copy-start(f32[2,1,3072]{2,1,0:T(1,128)S(1)} %reshape.37.ks_ref) | copy-start | bytes 73732
  43.2 0.8 copy-start.2

commit v5 on v4

--- a/solution.py
+++ b/solution.py
@@ -12,6 +12,9 @@
 GROUP = 8
 BLK = 128
 PAD_ROWS = 16
+HALVES = 2
+DEPTH = 4
+LAST = 2
 NEG_FILL = -1e30
 
 
@@ -146,7 +149,8 @@
     kv_local = qs_ref.shape[0]
     stride = chunks * BLK + PAD_ROWS
     features = weight.shape[2]
-    tile = math.gcd(features, 512)
+    span = features // HALVES
+    tile = math.gcd(span, 512)
     is_end = (me == 0) | (me == n - 1)
 
     def load_weight(d):
@@ -252,42 +256,48 @@
                     accum[h, :, :HD] / accum[h, :, HD:]
                 ).astype(jnp.bfloat16)
 
-    def products(c, d, use):
-        @pl.loop(0, features // tile)
+    def products(c, d, half, use):
+        @pl.loop(0, span // tile)
         def _(i):
             cols = pl.ds(pl.multiple_of(i * tile, tile), tile)
+            whole = pl.ds(pl.multiple_of(half * span + i * tile, tile), tile)
             use(
                 cols,
-                jnp.dot(attended[c], weight[d, :, cols], preferred_element_type=jnp.float32),
+                whole,
+                jnp.dot(attended[c], weight[d, :, whole], preferred_element_type=jnp.float32),
             )
 
-    def hop(c, d, up):
+    def hop(c, d, half, up):
         slot = d if up else jnp.where(d == me - 1, n, d)
         return pltpu.make_async_remote_copy(
-            src_ref=parts.at[c, d],
-            dst_ref=parts.at[c, slot],
-            send_sem=send_sem.at[c, d],
-            recv_sem=recv_sem.at[c, slot],
+            src_ref=parts.at[c, d, half],
+            dst_ref=parts.at[c, slot, half],
+            send_sem=send_sem.at[c, d, half],
+            recv_sem=recv_sem.at[c, slot, half],
             device_id={"head": me + 1 if up else me - 1},
             device_id_type=pl.DeviceIdType.MESH,
         )
 
-    def arrived(c, slot):
-        pltpu.make_async_copy(parts.at[c, slot], parts.at[c, slot], recv_sem.at[c, slot]).wait()
+    def arrived(c, slot, half):
+        piece = parts.at[c, slot, half]
+        pltpu.make_async_copy(piece, piece, recv_sem.at[c, slot, half]).wait()
 
     def count_of(up):
-        return n - 1 - me if up else me
+        return HALVES * (n - 1 - me if up else me)
 
     def nth(q, up):
         per = jnp.maximum(count_of(up), 1)
         k = lax.rem(q, per)
-        return hop(lax.div(q, per), n - 1 - k if up else k, up)
+        j = lax.div(k, HALVES)
+        return hop(lax.div(q, per), n - 1 - j if up else j, lax.rem(k, HALVES), up)
 
     def relay(c, k, up):
-        d = n - 1 - k if up else k
+        j = lax.div(k, HALVES)
+        half = lax.rem(k, HALVES)
+        d = n - 1 - j if up else j
         source = me > 0 if up else me < n - 1
 
-        @pl.when(c == 0)
+        @pl.when((c == 0) & (half == 0))
         def _():
             load_weight(d).wait()
 
@@ -297,44 +307,43 @@
 
         @pl.when(source)
         def _():
-            arrived(c, d)
-
-            def use(cols, product):
-                parts[c, d, :, cols] = (parts[c, d, :, cols].astype(jnp.float32) + product).astype(
-                    jnp.bfloat16
-                )
-
-            products(c, d, use)
+            arrived(c, d, half)
+
+            def use(cols, whole, product):
+                parts[c, d, half, :, cols] = (
+                    parts[c, d, half, :, cols].astype(jnp.float32) + product
+                ).astype(jnp.bfloat16)
+
+            products(c, d, half, use)
 
         @pl.when(jnp.logical_not(source))
         def _():
-            def use(cols, product):
-                parts[c, d, :, cols] = product.astype(jnp.bfloat16)
-
-            products(c, d, use)
+            def use(cols, whole, product):
+                parts[c, d, half, :, cols] = product.astype(jnp.bfloat16)
+
+            products(c, d, half, use)
 
         q = c * count_of(up) + k
-
         final = c == chunks - 1
 
-        @pl.when((q >= 2) & (jnp.logical_not(final) | (k == 0)))
-        def _():
-            nth(q - 2, up).wait_send()
-
-        @pl.when((q >= 1) & final)
-        def _():
-            nth(q - 1, up).wait_send()
+        @pl.when((q >= DEPTH) & (jnp.logical_not(final) | (k < LAST)))
+        def _():
+            nth(q - DEPTH, up).wait_send()
+
+        @pl.when((q >= LAST) & final)
+        def _():
+            nth(q - LAST, up).wait_send()
 
         nth(q, up).start()
 
     def forward(c):
         def ups():
-            @pl.loop(0, n - 1 - me)
+            @pl.loop(0, count_of(True))
             def _(k):
                 relay(c, k, True)
 
         def downs():
-            @pl.loop(0, me)
+            @pl.loop(0, count_of(False))
             def _(k):
                 relay(c, k, False)
 
@@ -373,19 +382,21 @@
         rows = pl.ds(pl.multiple_of(c * BLK, BLK), BLK)
 
         def finish(below, above):
-            if below:
-                arrived(c, me)
-            if above:
-                arrived(c, n)
-
-            def use(cols, product):
+            @pl.loop(0, HALVES)
+            def _(half):
                 if below:
-                    product = product + parts[c, me, :, cols].astype(jnp.float32)
+                    arrived(c, me, half)
                 if above:
-                    product = product + parts[c, n, :, cols].astype(jnp.float32)
-                o_ref[rows, cols] = (product * scale_ref[:, cols]).astype(jnp.bfloat16)
-
-            products(c, me, use)
+                    arrived(c, n, half)
+
+                def use(cols, whole, product):
+                    if below:
+                        product = product + parts[c, me, half, :, cols].astype(jnp.float32)
+                    if above:
+                        product = product + parts[c, n, half, :, cols].astype(jnp.float32)
+                    o_ref[rows, whole] = (product * scale_ref[:, whole]).astype(jnp.bfloat16)
+
+                products(c, me, half, use)
 
         @pl.when(me == 0)
         def _():
@@ -402,9 +413,9 @@
     for up in (True, False):
         total = chunks * count_of(up)
 
-        @pl.when(total > 0)
-        def _():
-            nth(total - 1, up).wait_send()
+        @pl.loop(jnp.maximum(total - LAST, 0), total)
+        def _(q):
+            nth(q, up).wait_send()
 
 
 def gather_kernel(ranks, x_ref, o_ref, own_sem, send_sem, pass_sem, recv_sem):
@@ -485,13 +496,13 @@
         scratch_shapes=[
             pltpu.VMEM((n, width, features), jnp.bfloat16),
             pltpu.VMEM((chunks, BLK, width), jnp.bfloat16),
-            pltpu.VMEM((chunks, n + 1, BLK, features), jnp.bfloat16),
+            pltpu.VMEM((chunks, n + 1, HALVES, BLK, features // HALVES), jnp.bfloat16),
             pltpu.VMEM((GROUP, BLK, HD), jnp.float32),
             pltpu.VMEM((GROUP, BLK, HD), jnp.float32),
             pltpu.VMEM((GROUP, BLK, 2 * HD), jnp.float32),
             pltpu.SemaphoreType.DMA((n,)),
-            pltpu.SemaphoreType.DMA((chunks, n)),
-            pltpu.SemaphoreType.DMA((chunks, n + 1)),
+            pltpu.SemaphoreType.DMA((chunks, n, HALVES)),
+            pltpu.SemaphoreType.DMA((chunks, n + 1, HALVES)),
         ],
         compiler_params=pltpu.CompilerParams(
             collective_id=0, has_side_effects=True, vmem_limit_bytes=60 * 2**20

time: 171 us -> 163 us (0.953)
  the two profiles are of different devices: /device:TPU:6 before, /device:TPU:31 now
where the time goes in v5:
time: 163 us; the launch traced here: 162 us
  Pallas kernels  149 us (91%)
  local copies, waits for them, and re-layouts  9.86 us (6%)
  other arithmetic  3.42 us (2%)
    pallas_call x1, Pallas kernels, project(): pl.pallas_call(functools.partial(project_kernel, n, ranks), out_shape=jax...  112 us
    pallas_call x1, Pallas kernels, gather(): pl.pallas_call(functools.partial(gather_kernel, ranks), out_shape=jax.Sha...  24.8 us
    pallas_call x1, Pallas kernels, attend(): pl.pallas_call(functools.partial(attend_kernel, per_rank), out_shape=jax....  11.9 us
    unnamed x13, local copies, waits for them, and re-layouts  5.45 us

profile of v5, /device:TPU:31, one launch (start us, length us, event | category | flops | bytes accessed | tf_op | source)
XLA Modules:
  0.0 162.0 jit_solution(17482721705930380890)
XLA Ops:
  0.0 0.0 copy-start.1
  0.0 0.0 copy-start.5
  0.0 0.8 constant_dynamic-slice_fusion
  0.8 0.7 reshape.30
  1.5 0.7 broadcast_in_dim.4
  2.2 0.9 copy.12
  3.1 0.0 copy-start.3
  3.1 0.8 copy.13
  3.9 0.5 mul.14
  4.4 1.0 fusion.2
  5.4 1.7 %fusion.1.x_ref = bf16[400,512]{1,0:T(8,128)(2,1)} fusion(bf16[6,128]{1,0:T(8,128)(2,1)S(1)} %reshape.30, bf16[384,256]{1,0:T(8,128)(2,1)S(1)} %fusion.2, bf16[384,256]{1,0:T(8,128)(2,1)} %param.11), kind=kLoop, calls=%fused_computation.2 | loop fusion | flops 1638400 | bytes 804352 | tf_op jit(solution)/shard_map/concatenate | solution.py:526
  7.1 24.8 %shard_map.91 = bf16[8,400,512]{2,1,0:T(8,128)(2,1)} custom-call(bf16[400,512]{1,0:T(8,128)(2,1)} %fusion.1.x_ref), custom_call_target="tpu_custom_call" | custom-call | tf_op jit(solution)/shard_map/pallas_call | solution.py:468
  31.9 0.7 slice_convert_fusion
  32.7 0.0 copy-done.1
  32.7 0.0 copy-done.5
  32.7 0.0 copy-start
  32.7 1.9 %copy-done = bf16[8,400,512]{2,1,0:T(8,128)(2,1)S(1)} copy-done((bf16[8,400,512]{2,1,0:T(8,128)(2,1)S(1)}, bf16[8,400,512]{2,1,0:T(8,128)(2,1)}, u32[]{:S(2)}) %copy-start) | copy-done | bytes 3276824
  34.6 0.0 copy-start.4
  34.6 11.9 %shard_map.92.first_ref = bf16[128,2048]{1,0:T(8,128)(2,1)S(1)} custom-call(s32[24,24]{1,0:T(8,128)S(1)} %copy-done.5, s32[1]{0:T(128)} %bitcast.rank_ref, bf16[384,2048]{1,0:T(8,128)(2,1)S(1)} %copy-done.1, bf16[2,384,8]{2,1,0:T(8,128)(2,1)S(1)} %bitcast.16, bf16[3200,512]{1,0:T(8,128)(2,1)S(1)} %bitcast.14, bf16[3200,512]{1,0:T(8,128)(2,1)S(1)} %bitcast.15, ...), custom_call_target="tpu_custom_call" | custom-call | tf_op jit(solution)/shard_map/pallas_call | solution.py:98
  46.5 0.0 copy-done.3
  46.5 0.0 copy-done.4
  46.5 0.0 copy-start.2
  46.5 0.8 copy-done.2
  47.3 112.0 %shard_map.93 = bf16[384,2048]{1,0:T(8,128)(2,1)} custom-call(bf16[128,2048]{1,0:T(8,128)(2,1)} %copy-done.2, bf16[384,2048]{1,0:T(8,128)(2,1)} %q_ref.3, bf16[2,384,8]{2,1,0:T(8,128)(2,1)} %bitcast.17, bf16[3200,512]{1,0:T(8,128)(2,1)} %bitcast.13, f32[2,1,3072]{2,1,0:T(1,128)} %copy-done.4, s32[3,1,3072]{2,1,0:T(1,128)} %bitcast.19, ...), custom_call_target="tpu_custom_call" | custom-call | tf_op jit(solution)/shard_map/pallas_call | solution.py:491
  159.3 2.7 %copy.18 = bf16[384,2048]{1,0:T(8,128)(2,1)} copy(bf16[384,2048]{1,0:T(8,128)(2,1)} %shard_map.93) | data formatting | bytes 3145728
  (3 shorter events, 0.0 us)
Async XLA Ops:
  0.0 32.7 %copy-start.1 = (bf16[384,2048]{1,0:T(8,128)(2,1)S(1)}, bf16[384,2048]{1,0:T(8,128)(2,1)}, u32[]{:S(2)}) copy-start(bf16[384,2048]{1,0:T(8,128)(2,1)} %q_ref.3) | copy-start | bytes 4718596
  0.0 32.7 %copy-start.5 = (s32[24,24]{1,0:T(8,128)S(1)}, s32[24,24]{1,0:T(8,128)}, u32[]{:S(2)}) copy-start(s32[24,24]{1,0:T(8,128)} %mask_ref.1) | copy-start | bytes 6916
  3.1 43.4 %copy-start.3 = (bf16[384,2,8]{2,0,1:T(8,128)(2,1)}, bf16[384,2,8]{2,0,1:T(8,128)(2,1)S(1)}, u32[]{:S(2)}) copy-start(bf16[384,2,8]{2,0,1:T(8,128)(2,1)S(1)} %copy.12) | copy-start | bytes 36868
  32.7 1.9 %copy-start = (bf16[8,400,512]{2,1,0:T(8,128)(2,1)S(1)}, bf16[8,400,512]{2,1,0:T(8,128)(2,1)}, u32[]{:S(2)}) copy-start(bf16[8,400,512]{2,1,0:T(8,128)(2,1)} %shard_map.91) | copy-start | bytes 9830404
  34.6 11.9 %copy-start.4 = (f32[2,1,3072]{2,1,0:T(1,128)}, f32[2,1,3072]{2,1,0:T(1,128)S(1)}, u32[]{:S(2)}) copy-start(f32[2,1,3072]{2,1,0:T(1,128)S(1)} %reshape.37.ks_ref) | copy-start | bytes 73732
  46.5 0.8 copy-start.2
